TPU v7x, 512 devices: a whole 4x4x16 slice. The times are simulated.
512 devices in a mesh: row: 16 (over z), col: 32 (over x, y, core).
Axes of the slice: x: 4, y: 4, z: 16, core: 2. Of those that a mesh axis runs over, the one named last changes fastest.
Arguments:
- pair: bfloat16 [1024, 1024, 128], P('row', 'col'), may hold values from -6 to 6
- pair_mask: int32 [1024, 1024], P('row', 'col'), may hold values from 0 to 1, as said below
- norm_gain: float32 [128], replicated, may hold values from 0.1 to 1.9
- norm_shift: float32 [128], replicated, may hold values from -3 to 3
- w_in: bfloat16 [128, 512], replicated, may hold values from -0.5 to 0.5
- out_gain: float32 [128], replicated, may hold values from 0.1 to 1.9
- out_shift: float32 [128], replicated, may hold values from -3 to 3
- w_out: bfloat16 [128, 128], replicated, may hold values from -0.5 to 0.5
- w_gate: bfloat16 [128, 128], replicated, may hold values from -0.5 to 0.5
Outputs:
- update: bfloat16 [1024, 1024, 128], P('row', 'col')
Inputs may be any that keep to these rules, and one draw needn't show every extreme that they name: pair_mask[i, j] = valid[i] * valid[j] for a 0/1 vector valid over the 1024 tokens; the last tokens of the crop (one or more) are padding with valid 0, and some other tokens are invalid too.
All inputs are finite; a program needn't handle non-finite values.
Results may differ from a plain program's by a relative error of at most 0.0058.
Values may be sent and summed in bfloat16 or wider, within the bound.
A program may use at most 64 MiB of HBM per device.

v0:
```python
import jax
import jax.numpy as jnp
from jax import lax
from jax.sharding import PartitionSpec as P

NORM_EPS = 1e-05


def partner(block, axis, stride):
    count = lax.axis_size(axis)
    route = []
    for low in range(count):
        high = low | 1 << stride
        if high != low and high < count:
            route += [(low, high), (high, low)]
    return lax.ppermute(block, axis, route)


def layer_norm(values, gain_vec, shift_vec, norm_axis):
    centre = jnp.mean(values, axis=norm_axis, keepdims=True)
    centred = values - centre
    second_moment = jnp.mean(centred * centred, axis=norm_axis, keepdims=True)
    return centred * lax.rsqrt(second_moment + NORM_EPS) * gain_vec + shift_vec


def ordered_join(own_part, theirs, upper_half, join_axis):
    leading = jnp.where(upper_half == 0, own_part, theirs)
    trailing = jnp.where(upper_half == 0, theirs, own_part)
    return jnp.concatenate([leading, trailing], axis=join_axis)


def on_device(pair, pair_mask, norm_gain, norm_shift, w_in, out_gain, out_shift, w_out, w_gate):
    row_block, col_block, channels = pair.shape
    col_count = lax.axis_size("col")
    total_bits = lax.axis_size("row").bit_length() - 1
    low_bits = 1
    row_place = lax.axis_index("row")
    flat_pair = pair.reshape(row_block * col_block, channels)
    normed = layer_norm(flat_pair.astype(jnp.float32), norm_gain, norm_shift, -1).astype(
        jnp.bfloat16
    )
    validity = pair_mask.reshape(1, row_block * col_block).astype(jnp.float32)
    linear = jnp.einsum("pc,cd->dp", normed, w_in, preferred_element_type=jnp.float32)
    linear = linear.reshape(4, channels, row_block * col_block)
    left_panel = (validity * jax.nn.sigmoid(linear[1]) * linear[0]).astype(jnp.bfloat16)
    right_panel = (validity * jax.nn.sigmoid(linear[3]) * linear[2]).astype(jnp.bfloat16)
    left_flat, right_flat = (
        lax.all_to_all(left_panel, "col", split_axis=0, concat_axis=1, tiled=True),
        lax.all_to_all(right_panel, "col", split_axis=0, concat_axis=1, tiled=True),
    )
    local_channels = left_flat.shape[0]

    def token_order(flat_rows):
        blocks = flat_rows.reshape(local_channels, col_count, row_block, col_block)
        return blocks.transpose(0, 2, 1, 3).reshape(
            local_channels, row_block, col_count * col_block
        )

    left_rows = token_order(left_flat)
    right_rows = token_order(right_flat)
    bit_number = 0
    partner_rows = partner(left_rows, "row", bit_number)
    left_rows = ordered_join(left_rows, partner_rows, row_place >> bit_number & 1, 1)
    for bit_number in range(low_bits, total_bits):
        partner_cols = partner(right_rows, "row", bit_number)
        right_rows = ordered_join(right_rows, partner_cols, row_place >> bit_number & 1, 1)
    products = jnp.einsum(
        "cik,cjk->cij", left_rows, right_rows, preferred_element_type=jnp.float32
    ).astype(jnp.bfloat16)
    group_size = 1 << low_bits
    j_span = right_rows.shape[1]
    holding = products.reshape(local_channels, group_size, row_block, 1, j_span)
    bit_number = 0
    remaining = holding.shape[1]
    q_count = holding.shape[3]
    halves = holding.reshape(local_channels, remaining // 2, 2, row_block, q_count, j_span)
    own_bit = row_place >> bit_number & 1
    retained = lax.dynamic_index_in_dim(halves, own_bit, axis=2, keepdims=False)
    outgoing = lax.dynamic_index_in_dim(halves, 1 - own_bit, axis=2, keepdims=False)
    incoming = partner(outgoing, "row", bit_number)
    leading = jnp.where(own_bit == 0, retained, incoming)
    trailing = jnp.where(own_bit == 0, incoming, retained)
    holding = jnp.stack([leading, trailing], axis=3).reshape(
        local_channels, remaining // 2, row_block, 2 * q_count, j_span
    )
    spread_rows = holding.reshape(
        local_channels, row_block, group_size, j_span // row_block, row_block
    )
    full_rows = spread_rows.transpose(0, 1, 3, 2, 4).reshape(
        local_channels, row_block, group_size * j_span
    )
    gathered = lax.all_to_all(full_rows, "col", split_axis=2, concat_axis=0, tiled=True)
    flat_out = gathered.reshape(channels, row_block * col_block).astype(jnp.float32)
    normed_out = layer_norm(flat_out, out_gain[:, None], out_shift[:, None], 0).astype(jnp.bfloat16)
    update = jnp.einsum("cp,cd->pd", normed_out, w_out, preferred_element_type=jnp.float32)
    gate_value = jax.nn.sigmoid(jnp.dot(normed, w_gate, preferred_element_type=jnp.float32))
    return (gate_value * update).astype(jnp.bfloat16).reshape(row_block, col_block, channels)


def solution(mesh):
    in_specs = (P("row", "col", None), P("row", "col"), P(), P(), P(), P(), P(), P(), P())
    out_specs = P("row", "col", None)
    return jax.shard_map(
        on_device, mesh=mesh, in_specs=in_specs, out_specs=out_specs, check_vma=False
    )
```

profile of v0, /device:TPU:1, one launch (start us, length us, event | category | flops | bytes accessed | tf_op | source)
XLA Modules:
  0.0 460.6 jit_solution(16014749891169446794)
XLA Ops:
  0.0 1.4 convert_reduce_fusion
  1.4 1.7 multiply_reduce_fusion.1
  3.1 0.1 div.34
  3.2 0.1 rsqrt.23
  3.3 1.7 fusion.24
  5.0 0.0 copy-start.1
  5.0 0.8 copy-done.1
  5.8 0.7 convolution_bitcast_fusion
  6.5 1.8 fusion.17
  8.3 0.3 div.38
  8.6 0.3 div.40
  8.9 0.0 copy-start.6
  9.0 1.5 squeeze.15
  10.5 2.5 squeeze.16
  13.0 0.1 copy.65
  13.1 0.1 convert_element_type.64
  13.2 2.9 multiply_convert_fusion.1
  16.1 21.2 %all_to_all.35 = bf16[32,4,2048]{2,1,0:T(4,128)(2,1)S(1)} all-to-all(bf16[32,4,2048]{2,1,0:T(4,128)(2,1)S(1)} %get-tuple-element.22), channel_id=1, replica_groups=mesh['row'=16,'col'=32] {'col'}, dimensions={0} | all-to-all | bytes 1048576 | tf_op jit(solution)/shard_map/all_to_all | solution.py:49
  37.3 0.3 copy.71
  37.6 1.6 reshape.155
  39.3 0.9 copy.72
  40.2 0.3 copy.74
  40.6 3.7 collective-permute-start.1
  44.3 24.0 %collective-permute-done.1 = bf16[4,64,1024]{2,1,0:T(8,128)(2,1)S(1)} collective-permute-done((bf16[4,64,1024]{2,1,0:T(8,128)(2,1)S(1)}, bf16[4,64,1024]{2,1,0:T(8,128)(2,1)S(1)}, u32[]{:S(2)}, u32[]{:S(2)}) %collective-permute-start.1) | collective-permute-done | bytes 524320 | tf_op jit(solution)/shard_map/ppermute | solution.py:16
  68.3 0.1 broadcast_select_fusion.5
  68.4 0.1 pad_maximum_fusion.1
  68.4 8.4 %collective-permute-start.2 = (bf16[4,128,1024]{2,1,0:T(8,128)(2,1)S(1)}, bf16[4,128,1024]{2,1,0:T(8,128)(2,1)}, u32[]{:S(2)}, u32[]{:S(2)}) collective-permute-start(bf16[4,128,1024]{2,1,0:T(8,128)(2,1)S(1)} %pad_maximum_fusion.1), channel_id=1, source_target_pairs={{0,128},{128,0},{32,160},{160,32},{64,192},{192,64},{96,224},{224,... | collective-permute-start | bytes 3145736 | tf_op jit(solution)/shard_map/ppermute | solution.py:16
  76.9 135.4 %collective-permute-done.2 = bf16[4,128,1024]{2,1,0:T(8,128)(2,1)} collective-permute-done((bf16[4,128,1024]{2,1,0:T(8,128)(2,1)S(1)}, bf16[4,128,1024]{2,1,0:T(8,128)(2,1)}, u32[]{:S(2)}, u32[]{:S(2)}) %collective-permute-start.2) | collective-permute-done | bytes 1048608 | tf_op jit(solution)/shard_map/ppermute | solution.py:16
  212.3 1.8 broadcast_select_fusion.3
  214.1 1.5 pad_maximum_fusion
  215.6 102.6 %collective-permute-start.3 = (bf16[4,256,1024]{2,1,0:T(8,128)(2,1)}, bf16[4,256,1024]{2,1,0:T(8,128)(2,1)}, u32[]{:S(2)}, u32[]{:S(2)}) collective-permute-start(bf16[4,256,1024]{2,1,0:T(8,128)(2,1)} %pad_maximum_fusion), channel_id=1, source_target_pairs={{0,256},{256,0},{32,288},{288,32},{64,320},{320,64},{96,352},{352,... | collective-permute-start | bytes 6291464 | tf_op jit(solution)/shard_map/ppermute | solution.py:16
  318.2 15.9 %all_to_all.36 = bf16[32,4,2048]{2,1,0:T(4,128)(2,1)S(1)} all-to-all(bf16[32,4,2048]{2,1,0:T(4,128)(2,1)S(1)} %copy-done.3), channel_id=1, replica_groups=mesh['row'=16,'col'=32] {'col'}, dimensions={0} | all-to-all | bytes 1048576 | tf_op jit(solution)/shard_map/all_to_all | solution.py:48
  334.1 0.3 copy.66
  334.4 2.6 reshape.153
  337.0 2.0 copy.67
  339.1 1.1 copy.69
  340.2 2.1 collective-permute-start
  342.3 70.7 %collective-permute-done = bf16[4,64,1024]{2,1,0:T(8,128)(2,1)S(1)} collective-permute-done((bf16[4,64,1024]{2,1,0:T(8,128)(2,1)}, bf16[4,64,1024]{2,1,0:T(8,128)(2,1)S(1)}, u32[]{:S(2)}, u32[]{:S(2)}) %collective-permute-start) | collective-permute-done | bytes 524320 | tf_op jit(solution)/shard_map/ppermute | solution.py:16
  413.0 1.1 broadcast_select_fusion.7
  414.2 2.8 broadcast_select_fusion.1
  416.9 1.7 fusion.8
  418.6 4.0 collective-permute-start.4
  422.7 5.2 %collective-permute-done.4 = bf16[4,1,64,1,512]{4,2,0,3,1:T(8,128)(2,1)S(1)} collective-permute-done((bf16[4,1,64,1,512]{4,2,0,3,1:T(8,128)(2,1)S(1)}, bf16[4,1,64,1,512]{4,2,0,3,1:T(8,128)(2,1)S(1)}, u32[]{:S(2)}, u32[]{:S(2)}) %collective-permute-start.4) | collective-permute-done | bytes 262176 | tf_op jit(solution)/shard_map/ppermute | solution.py:16
  427.9 0.3 stack.10
  428.2 0.3 stack.9
  428.5 0.2 maximum_bitcast_fusion
  428.7 0.0 copy-start.2
  428.7 1.0 copy.83
  429.7 1.5 reshape.163
  431.3 5.6 %all-to-all-start.2 = ((bf16[32,2,4096]{2,1,0:T(2,128)(2,1)}), bf16[32,2,4096]{2,1,0:T(2,128)(2,1)S(1)}, u32[]{:S(2)}, u32[]{:S(2)}) async-start(bf16[32,2,4096]{2,1,0:T(2,128)(2,1)} %reshape.163), calls=%async_computation.2 | async-start | bytes 1048576 | tf_op jit(solution)/shard_map/all_to_all | solution.py:92
  436.9 1.4 fusion.6
  438.3 10.3 %all-to-all-done.2 = bf16[32,2,4096]{2,1,0:T(2,128)(2,1)S(1)} async-done(((bf16[32,2,4096]{2,1,0:T(2,128)(2,1)}), bf16[32,2,4096]{2,1,0:T(2,128)(2,1)S(1)}, u32[]{:S(2)}, u32[]{:S(2)}) %all-to-all-start.2) | async-done | bytes 524320 | tf_op jit(solution)/shard_map/all_to_all | solution.py:92
  448.6 1.6 reshape.164
  450.3 1.5 fusion.30
  451.8 0.3 fusion.11
  452.0 0.1 copy.80
  452.1 0.1 copy.81
  452.2 0.1 div.42
  452.2 0.4 multiply_reduce_fusion
  452.6 0.1 copy.82
  452.7 0.1 rsqrt.25
  452.8 2.7 copy.79
  455.6 3.7 reshape.160
  459.3 1.2 fusion.7
  (24 shorter events, 0.2 us)
Async XLA Ops:
  0.0 5.8 %copy-start = (bf16[128,512]{1,0:T(8,128)(2,1)S(1)}, bf16[128,512]{1,0:T(8,128)(2,1)}, u32[]{:S(2)}) copy-start(bf16[128,512]{1,0:T(8,128)(2,1)} %param.13) | copy-start | bytes 393220
  5.0 0.8 copy-start.1
  8.9 4.1 copy-start.6
  40.6 27.7 %collective-permute-start.1 = (bf16[4,64,1024]{2,1,0:T(8,128)(2,1)S(1)}, bf16[4,64,1024]{2,1,0:T(8,128)(2,1)S(1)}, u32[]{:S(2)}, u32[]{:S(2)}) collective-permute-start(bf16[4,64,1024]{2,1,0:T(8,128)(2,1)S(1)} %copy.74), channel_id=1, source_target_pairs={{0,64},{64,0},{32,96},{96,32},{128,192},{192,128},{160,224},{224,1... | collective-permute-start | bytes 1572872 | tf_op jit(solution)/shard_map/ppermute | solution.py:16
  68.4 143.8 %collective-permute-start.2 = (bf16[4,128,1024]{2,1,0:T(8,128)(2,1)S(1)}, bf16[4,128,1024]{2,1,0:T(8,128)(2,1)}, u32[]{:S(2)}, u32[]{:S(2)}) collective-permute-start(bf16[4,128,1024]{2,1,0:T(8,128)(2,1)S(1)} %pad_maximum_fusion.1), channel_id=1, source_target_pairs={{0,128},{128,0},{32,160},{160,32},{64,192},{192,64},{96,224},{224,... | collective-permute-start | bytes 3145736 | tf_op jit(solution)/shard_map/ppermute | solution.py:16
  214.1 104.1 %copy-start.3 = (bf16[32,4,2048]{2,1,0:T(4,128)(2,1)S(1)}, bf16[32,4,2048]{2,1,0:T(4,128)(2,1)}, u32[]{:S(2)}) copy-start(bf16[32,4,2048]{2,1,0:T(4,128)(2,1)} %get-tuple-element.21) | copy-start | bytes 1572868
  215.6 198.6 %collective-permute-start.3 = (bf16[4,256,1024]{2,1,0:T(8,128)(2,1)}, bf16[4,256,1024]{2,1,0:T(8,128)(2,1)}, u32[]{:S(2)}, u32[]{:S(2)}) collective-permute-start(bf16[4,256,1024]{2,1,0:T(8,128)(2,1)} %pad_maximum_fusion), channel_id=1, source_target_pairs={{0,256},{256,0},{32,288},{288,32},{64,320},{320,64},{96,352},{352,... | collective-permute-start | bytes 6291464 | tf_op jit(solution)/shard_map/ppermute | solution.py:16
  340.2 72.9 %collective-permute-start = (bf16[4,64,1024]{2,1,0:T(8,128)(2,1)}, bf16[4,64,1024]{2,1,0:T(8,128)(2,1)S(1)}, u32[]{:S(2)}, u32[]{:S(2)}) collective-permute-start(bf16[4,64,1024]{2,1,0:T(8,128)(2,1)} %copy.69), channel_id=1, source_target_pairs={{0,32},{32,0},{64,96},{96,64},{128,160},{160,128},{192,224},{224,1... | collective-permute-start | bytes 1572872 | tf_op jit(solution)/shard_map/ppermute | solution.py:16
  418.6 9.2 %collective-permute-start.4 = (bf16[4,1,64,1,512]{4,2,0,3,1:T(8,128)(2,1)S(1)}, bf16[4,1,64,1,512]{4,2,0,3,1:T(8,128)(2,1)S(1)}, u32[]{:S(2)}, u32[]{:S(2)}) collective-permute-start(bf16[4,1,64,1,512]{4,2,0,3,1:T(8,128)(2,1)S(1)} %dynamic-slice_bitcast_fusion), channel_id=1, source_target_pairs={{0,32},{32,0},{64,96},{96,64},{128,160},{160,128},{192,224},{224,1... | collective-permute-start | bytes 786440 | tf_op jit(solution)/shard_map/ppermute | solution.py:16
  428.7 8.2 %copy-start.2 = (bf16[2048,128]{1,0:T(8,128)(2,1)S(1)}, bf16[2048,128]{1,0:T(8,128)(2,1)}, u32[]{:S(2)}) copy-start(bf16[2048,128]{1,0:T(8,128)(2,1)} %copy-done.1) | copy-start | bytes 1572868
  428.7 8.2 %copy-start.9 = (bf16[128,128]{1,0:T(8,128)(2,1)S(1)}, bf16[128,128]{1,0:T(8,128)(2,1)}, u32[]{:S(2)}) copy-start(bf16[128,128]{1,0:T(8,128)(2,1)} %param.17) | copy-start | bytes 98308
  431.3 17.3 %all-to-all-start.2 = ((bf16[32,2,4096]{2,1,0:T(2,128)(2,1)}), bf16[32,2,4096]{2,1,0:T(2,128)(2,1)S(1)}, u32[]{:S(2)}, u32[]{:S(2)}) async-start(bf16[32,2,4096]{2,1,0:T(2,128)(2,1)} %reshape.163), calls=%async_computation.2 | async-start | bytes 1048576 | tf_op jit(solution)/shard_map/all_to_all | solution.py:92
  455.5 3.8 copy-start.4
  455.5 3.8 copy-start.5
  455.6 3.8 copy-start.7
  455.6 3.8 copy-start.8
where the time goes:
time: 461 us
  waiting for transfers between devices  246 us (53%)
  starting transfers between devices  126 us (27%)
  blocking collectives  37.2 us (8%)
  local copies, waits for them, and re-layouts  26.7 us (6%)
  other arithmetic  19.3 us (4%)
  matrix products  5.04 us (1%)
    ppermute x5, waiting for transfers between devices, partner(): return lax.ppermute(block, axis, route)  235 us
    ppermute x5, starting transfers between devices, partner(): return lax.ppermute(block, axis, route)  121 us
    all_to_all x1, blocking collectives, on_device(): lax.all_to_all(right_panel, 'col', split_axis=0, concat_axis=1, tiled=True)  21.2 us
    all_to_all x1, blocking collectives, on_device(): lax.all_to_all(left_panel, 'col', split_axis=0, concat_axis=1, tiled=True)  15.9 us
    all_to_all x1, waiting for transfers between devices, on_device(): lax.all_to_all(full_rows, 'col', split_axis=2, concat_axis=0, tiled=True)  10.3 us
  transfers between devices with their start and end apart: 6, of which 5 were waited for; matrix products, arithmetic and copies ran while one was open for 2% of the time, Pallas kernels for 0%

commit v1 on v0

v1 whole, which is shorter than its diff:
```python
import jax
import jax.numpy as jnp
from jax import lax
from jax.experimental import pallas as pl
from jax.experimental.pallas import tpu as pltpu
from jax.sharding import PartitionSpec as P

NORM_EPS = 1e-05
MESH = pl.DeviceIdType.MESH
ROWS, COLS = 16, 32
F32, BF16 = jnp.float32, jnp.bfloat16
BLOCK_ORDER = (0, 2, 1, 3)


def place(z, shift, lean):
    left = lax.rem(z - shift + 34 - lean, ROWS)
    right = lax.rem(z - shift + 22 - lean, ROWS)
    return left // 8, lax.rem(left, 8), right // 8, lax.rem(right, 8)


def plane_of(shift, left_half, right_half):
    corner = jnp.where(left_half == 0, right_half, 3 - right_half)
    return lax.rem(shift + 4 * corner, ROWS)


def body(
    pair, mask, norm_gain, norm_shift, w_in, out_gain, out_shift, w_out, w_gate,
    update,
    normed, wide_left, wide_right, w_turned, mask_rows, left_own, right_own,
    left_col, right_col, right_turned, left_in, right_in, tiles, tiles_in, gathered, wide_out, gate,
    gain_col, shift_col,
    send_left, send_right, recv_left, recv_right, send_z, recv_zl, recv_zr, send_t, recv_t, send_o, recv_o,
):
    z, d = lax.axis_index("row"), lax.axis_index("col")
    core = lax.rem(d, 2)

    barrier = pltpu.get_barrier_semaphore()

    def greet_row(s, carry):
        pl.semaphore_signal(barrier, inc=1, device_id=(lax.rem(z + s, ROWS), d), device_id_type=MESH)
        return carry

    def greet_col(s, carry):
        pl.semaphore_signal(barrier, inc=1, device_id=(z, lax.rem(d + s, COLS)), device_id_type=MESH)
        return carry

    lax.fori_loop(1, ROWS, greet_row, 0)
    lax.fori_loop(1, COLS, greet_col, 0)

    def norm_rows(t, carry):
        rows = pl.ds(pl.multiple_of(t * 256, 256), 256)
        x = pair[rows, :].astype(F32)
        centred = x - jnp.mean(x, axis=-1, keepdims=True)
        second = jnp.mean(centred * centred, axis=-1, keepdims=True)
        normed[rows, :] = centred * lax.rsqrt(second + NORM_EPS) * norm_gain[...] + norm_shift[...]
        return carry

    lax.fori_loop(0, 8, norm_rows, 0)
    w_turned[...] = w_in[...].astype(F32).T.astype(BF16)
    valid = mask[...].astype(F32)
    valid = jnp.concatenate([valid[16 * b : 16 * b + 16] for b in BLOCK_ORDER], axis=0).T
    mask_rows[...] = jnp.concatenate([valid[0:16], valid[16:32]], axis=1)

    def panel_step(kk, carry):
        pieces = [
            normed[pl.ds(b * 512 + k2 * 16 + kk, 16, stride=32), :] for k2 in range(2) for b in BLOCK_ORDER
        ]
        x = jnp.concatenate(pieces, axis=0).astype(BF16)
        linear = lax.dot_general(w_turned[...], x, (((1,), (1,)), ((), ())), preferred_element_type=F32)
        m = mask_rows[pl.ds(kk, 1), :]
        wide_left[pl.ds(kk, 128, stride=16), :] = m * jax.nn.sigmoid(linear[128:256]) * linear[0:128]
        wide_right[pl.ds(kk, 128, stride=16), :] = m * jax.nn.sigmoid(linear[384:512]) * linear[256:384]
        return carry

    lax.fori_loop(0, 16, panel_step, 0)
    left_own[...] = wide_left[...].astype(BF16).reshape(128, 16, 128)
    right_own[...] = wide_right[...].astype(BF16).reshape(128, 16, 128)

    pl.semaphore_wait(barrier, ROWS + COLS - 2)

    def spread(own, col, send, recv):
        def one(s, carry):
            to = lax.rem(d + s, COLS)
            pltpu.make_async_remote_copy(
                src_ref=own.at[pl.ds(4 * to, 4)], dst_ref=col.at[:, pl.ds(d * 16, 16), :],
                send_sem=send, recv_sem=recv, device_id=(z, to), device_id_type=MESH,
            ).start()
            return carry

        lax.fori_loop(1, COLS, one, 0)
        pltpu.make_async_copy(own.at[pl.ds(4 * d, 4)], col.at[:, pl.ds(d * 16, 16), :], recv).start()

    spread(left_own, left_col, send_left, recv_left)
    spread(right_own, right_col, send_right, recv_right)

    def left_copy(q, s):
        shift = q + 4 * core
        half, slot, _, _ = place(z, shift, core)
        to = plane_of(shift, half, s)
        return to, left_col.at[q], left_in.at[slot], send_z.at[2 * q + s], recv_zl

    def right_copy(q, s):
        shift = q + 4 * core
        _, _, half, slot = place(z, shift, core)
        to = plane_of(shift, s, half)
        return to, right_turned.at[q], right_in.at[slot], send_z.at[8 + 2 * q + s], recv_zr.at[slot]

    def launch(to, src, dst, send, recv):
        @pl.when(to != z)
        def _():
            pltpu.make_async_remote_copy(
                src_ref=src, dst_ref=dst, send_sem=send, recv_sem=recv, device_id=(to, d), device_id_type=MESH
            ).start()

        @pl.when(to == z)
        def _():
            pltpu.make_async_copy(src, dst, recv).start()

    def landed(to, src, dst, send, recv):
        @pl.when(to != z)
        def _():
            pltpu.make_async_remote_copy(
                src_ref=src, dst_ref=dst, send_sem=send, recv_sem=recv, device_id=(to, d), device_id_type=MESH
            ).wait_send()

    pltpu.make_async_copy(left_col, left_col, recv_left).wait()
    for q in range(4):
        for s in range(2):
            launch(*left_copy(q, s))
    pltpu.make_async_copy(right_col, right_col, recv_right).wait()
    for q in range(4):
        right_turned[q] = right_col[q].astype(F32).T.astype(BF16)
        for s in range(2):
            launch(*right_copy(q, s))

    def gate_rows(t, carry):
        rows = pl.ds(pl.multiple_of(t * 256, 256), 256)
        gate[rows, :] = jax.nn.sigmoid(
            jnp.dot(normed[rows, :].astype(BF16), w_gate[...], preferred_element_type=F32)
        )
        return carry

    lax.fori_loop(0, 8, gate_rows, 0)
    gain_col[...] = jnp.broadcast_to(out_gain[...], (128, 128)).T
    shift_col[...] = jnp.broadcast_to(out_shift[...], (128, 128)).T

    my_q = lax.rem(z, 4)
    my_shift = my_q + 4 * core
    corner = lax.rem(z - my_shift + 16, ROWS) // 4
    my_left = corner // 2
    my_right = jnp.where(my_left == 0, corner, 3 - corner)
    left_base = lax.rem(my_shift - 2 + core + 8 * my_left + 16, ROWS)
    right_base = lax.rem(my_shift + 10 + core + 8 * my_right, ROWS)

    lanes_low = lax.broadcasted_iota(jnp.int32, (32, 128), 1) < 64

    def tile_copy(slot, a):
        to = lax.rem(left_base + a, ROWS)
        block = lax.rem(right_base + slot, ROWS)
        return (
            to, tiles.at[slot, a], tiles_in.at[my_q, pl.ds(2 * block, 2)], send_t, recv_t
        )

    pltpu.make_async_copy(left_in, left_in, recv_zl).wait()

    def multiply(slot, carry):
        pltpu.make_async_copy(right_in.at[slot], right_in.at[slot], recv_zr.at[slot]).wait()
        for pair_index in range(4):
            both = jnp.concatenate([left_in[2 * pair_index], left_in[2 * pair_index + 1]], axis=1)
            grid = jnp.dot(right_in[slot], both, preferred_element_type=F32)
            for side in range(2):
                m = grid[:, 128 * side : 128 * side + 128]
                kept = jnp.where(lanes_low, m[0:32], m[96:128])
                moved = jnp.where(lanes_low, m[32:64], m[64:96])
                tile = (kept + pltpu.roll(moved, 64, axis=1)).astype(BF16)
                tiles[slot, 2 * pair_index + side] = tile.reshape(2, 16, 128)
        for a in range(8):
            launch(*tile_copy(slot, a))
        return carry

    lax.fori_loop(0, 8, multiply, 0)

    pltpu.make_async_copy(tiles_in, tiles_in, recv_t).wait()

    def return_one(s, carry):
        to = lax.rem(d + s, COLS)
        pltpu.make_async_remote_copy(
            src_ref=tiles_in.at[:, to], dst_ref=gathered.at[pl.ds(4 * d, 4)],
            send_sem=send_o, recv_sem=recv_o, device_id=(z, to), device_id_type=MESH,
        ).start()
        return carry

    lax.fori_loop(1, COLS, return_one, 0)
    pltpu.make_async_copy(tiles_in.at[:, d], gathered.at[pl.ds(4 * d, 4)], recv_o).start()

    pltpu.make_async_copy(left_own.at[pl.ds(0, 124)], left_own.at[pl.ds(0, 124)], send_left).wait()
    pltpu.make_async_copy(right_own.at[pl.ds(0, 124)], right_own.at[pl.ds(0, 124)], send_right).wait()
    for q in range(4):
        for s in range(2):
            landed(*left_copy(q, s))
            landed(*right_copy(q, s))

    def tile_left(slot, carry):
        for a in range(8):
            landed(*tile_copy(slot, a))
        return carry

    lax.fori_loop(0, 8, tile_left, 0)

    pltpu.make_async_copy(gathered, gathered, recv_o).wait()

    def total(t, carry):
        block = gathered[pl.ds(8 * t, 8)].astype(F32)
        return carry + jnp.sum(block, axis=0)

    centre = lax.fori_loop(0, 16, total, jnp.zeros((16, 128), F32)) * (1.0 / 128)

    def squares(t, carry):
        block = gathered[pl.ds(8 * t, 8)].astype(F32) - centre[None]
        return carry + jnp.sum(block * block, axis=0)

    second = lax.fori_loop(0, 16, squares, jnp.zeros((16, 128), F32)) * (1.0 / 128)
    scale = lax.rsqrt(second + NORM_EPS)

    def centre_rows(t, carry):
        block = (gathered[pl.ds(8 * t, 8)].astype(F32) - centre[None]) * scale[None]
        wide_out[pl.ds(pl.multiple_of(t * 128, 128), 128), :] = block.reshape(128, 128)
        return carry

    lax.fori_loop(0, 16, centre_rows, 0)

    def project(jj, carry):
        x = wide_out[pl.ds(jj, 128, stride=16), :] * gain_col[...] + shift_col[...]
        out = jnp.dot(x.T.astype(BF16), w_out[...], preferred_element_type=F32)
        for j2 in range(2):
            for s, b in enumerate(BLOCK_ORDER):
                rows = pl.ds(b * 512 + j2 * 16 + jj, 16, stride=32)
                gate[rows, :] = gate[rows, :] * out[64 * j2 + 16 * s : 64 * j2 + 16 * s + 16]
        return carry

    lax.fori_loop(0, 16, project, 0)
    update[...] = gate[...].astype(BF16)

    pltpu.make_async_copy(tiles_in.at[:, pl.ds(0, 31)], tiles_in.at[:, pl.ds(0, 31)], send_o).wait()


def on_device(pair, pair_mask, norm_gain, norm_shift, w_in, out_gain, out_shift, w_out, w_gate):
    vmem = pl.BlockSpec(memory_space=pltpu.VMEM)
    dma = pltpu.SemaphoreType.DMA
    out = pl.pallas_call(
        body,
        out_shape=jax.ShapeDtypeStruct((2048, 128), BF16),
        in_specs=[vmem] * 9,
        out_specs=vmem,
        scratch_shapes=[
            pltpu.VMEM((2048, 128), F32),
            pltpu.VMEM((2048, 128), F32),
            pltpu.VMEM((2048, 128), F32),
            pltpu.VMEM((512, 128), BF16),
            pltpu.VMEM((16, 128), F32),
            pltpu.VMEM((128, 16, 128), BF16),
            pltpu.VMEM((128, 16, 128), BF16),
            pltpu.VMEM((4, 512, 128), BF16),
            pltpu.VMEM((4, 512, 128), BF16),
            pltpu.VMEM((4, 128, 512), BF16),
            pltpu.VMEM((8, 512, 128), BF16),
            pltpu.VMEM((8, 128, 512), BF16),
            pltpu.VMEM((8, 8, 2, 16, 128), BF16),
            pltpu.VMEM((4, 32, 16, 128), BF16),
            pltpu.VMEM((128, 16, 128), BF16),
            pltpu.VMEM((2048, 128), F32),
            pltpu.VMEM((2048, 128), F32),
            pltpu.VMEM((128, 128), F32),
            pltpu.VMEM((128, 128), F32),
            dma, dma, dma, dma,
            dma((16,)), dma, dma((8,)),
            dma, dma, dma, dma,
        ],
        compiler_params=pltpu.CompilerParams(
            collective_id=0, has_side_effects=True, vmem_limit_bytes=40 << 20
        ),
    )(
        pair.reshape(2048, 128), pair_mask, norm_gain.reshape(1, 128), norm_shift.reshape(1, 128), w_in,
        out_gain.reshape(1, 128), out_shift.reshape(1, 128), w_out, w_gate,
    )
    return out.reshape(64, 32, 128)


def solution(mesh):
    in_specs = (P("row", "col", None), P("row", "col"), P(), P(), P(), P(), P(), P(), P())
    out_specs = P("row", "col", None)
    return jax.shard_map(on_device, mesh=mesh, in_specs=in_specs, out_specs=out_specs, check_vma=False)
```

time: 461 us -> 126 us (0.27)
  waiting for transfers between devices: 246 us -> 0 us
  starting transfers between devices: 126 us -> 0 us
  Pallas kernels: 0 us -> 121 us
  blocking collectives: 37.2 us -> 0 us
  local copies, waits for them, and re-layouts: 26.7 us -> 4.36 us
  other arithmetic: 19.3 us -> 0 us
  matrix products: 5.04 us -> 0 us
    ppermute x5 -> x0, waiting for transfers between devices: 235 us -> none  [partner(): return lax.ppermute(block, axis, route)]
    pallas_call x0 -> x1, Pallas kernels: none -> 121 us  [on_device(): pl.pallas_call(body, out_shape=jax.ShapeDtypeStruct((2048, 128), BF16), i...]
    ppermute x5 -> x0, starting transfers between devices: 121 us -> none  [partner(): return lax.ppermute(block, axis, route)]
    all_to_all x2 -> x0, blocking collectives: 37.2 us -> none  [the longest x1 21.2 us: on_device(): lax.all_to_all(right_panel, 'col', split_axis=0, concat_axis=1, tiled=True)]
    all_to_all x1 -> x0, waiting for transfers between devices: 10.3 us -> none  [on_device(): lax.all_to_all(full_rows, 'col', split_axis=2, concat_axis=0, tiled=True)]
    reshape x5 -> x0, local copies, waits for them, and re-layouts: 6.73 us -> none  [the longest x2 4.27 us: token_order(): blocks = flat_rows.reshape(local_channels, col_count, row_block, col_block)]
    convert_element_type x4 -> x0, local copies, waits for them, and re-layouts: 6.62 us -> none  [the longest x2 6.46 us: on_device(): gathered.reshape(channels, row_block * col_block).astype(jnp.float32)]
    select_n x5 -> x0, other arithmetic: 5.77 us -> none  [the longest x4 5.73 us: ordered_join(): leading = jnp.where(upper_half == 0, own_part, theirs)]
  transfers between devices with their start and end apart: 6 -> 0, of which waited for: 5 -> 0; matrix products, arithmetic and copies ran while one was open for 2% -> 0% of each run, Pallas kernels for 0% -> 0%
where the time goes in v1:
time: 126 us; the launch traced here: 125 us
  Pallas kernels  121 us (96%)
  local copies, waits for them, and re-layouts  4.36 us (3%)
    pallas_call x1, Pallas kernels, on_device(): pl.pallas_call(body, out_shape=jax.ShapeDtypeStruct((2048, 128), BF16), i...  121 us
    unnamed x18, local copies, waits for them, and re-layouts  4.36 us

profile of v1, /device:TPU:1, one launch (start us, length us, event | category | flops | bytes accessed | tf_op | source)
XLA Modules:
  0.0 125.5 jit_solution(160688438366141449)
XLA Ops:
  0.0 0.0 copy-start.2
  0.0 0.0 copy-start.4
  0.0 0.0 copy-start.5
  0.0 0.0 copy-start.6
  0.0 0.0 copy-start.7
  0.0 0.8 copy.10.mask
  0.9 0.0 copy-done.2
  0.9 0.0 copy-done.4
  0.9 0.0 copy-done.5
  0.9 0.0 copy-done.6
  0.9 0.0 copy-done.7
  0.9 0.0 copy-start
  0.9 1.0 copy-done
  2.0 0.0 copy-start.1
  2.0 0.9 copy-done.1
  2.9 0.0 copy-start.3
  2.9 0.8 copy-done.3
  3.6 121.0 %shard_map.91 = bf16[2048,128]{1,0:T(8,128)(2,1)S(1)} custom-call(bf16[2048,128]{1,0:T(8,128)(2,1)S(1)} %bitcast.7, s32[64,32]{1,0:T(8,128)S(1)} %copy.10.mask, f32[1,128]{1,0:T(1,128)S(1)} %bitcast.8, f32[1,128]{1,0:T(1,128)S(1)} %bitcast.9, bf16[128,512]{1,0:T(8,128)(2,1)S(1)} %copy-done.1, f32[1,128]{1,0:T(1,128)S(1)} %bitcast.10, f32[1,128]{1,0:T(1,128)S(1)} %bitcast.11, ...), custom_call_target="tpu_custom_call" | custom-call | tf_op jit(solution)/shard_map/pallas_call | solution.py:250
  124.7 0.8 copy.12
Async XLA Ops:
  0.0 0.9 copy-start.2
  0.0 0.9 copy-start.4
  0.0 0.9 copy-start.5
  0.0 0.9 copy-start.6
  0.0 0.9 copy-start.7
  0.9 1.0 copy-start
  2.0 0.9 copy-start.1
  2.9 0.8 copy-start.3

commit v2 on v1

--- a/solution.py
+++ b/solution.py
@@ -24,8 +24,9 @@
 
 
 def body(
-    pair, mask, norm_gain, norm_shift, w_in, out_gain, out_shift, w_out, w_gate,
+    pair_hbm, mask_hbm, norm_gain_hbm, norm_shift_hbm, w_in_hbm, out_gain_hbm, out_shift_hbm, w_out_hbm, w_gate_hbm,
     update,
+    pair, mask, norm_gain, norm_shift, w_in, out_gain, out_shift, w_out, w_gate, load,
     normed, wide_left, wide_right, w_turned, mask_rows, left_own, right_own,
     left_col, right_col, right_turned, left_in, right_in, tiles, tiles_in, gathered, wide_out, gate,
     gain_col, shift_col,
@@ -34,6 +35,14 @@
     z, d = lax.axis_index("row"), lax.axis_index("col")
     core = lax.rem(d, 2)
 
+    operands = (
+        (pair_hbm, pair), (mask_hbm, mask), (norm_gain_hbm, norm_gain), (norm_shift_hbm, norm_shift), (w_in_hbm, w_in),
+        (out_gain_hbm, out_gain), (out_shift_hbm, out_shift), (w_out_hbm, w_out), (w_gate_hbm, w_gate),
+    )
+    loads = [pltpu.make_async_copy(src, dst, load.at[n]) for n, (src, dst) in enumerate(operands)]
+    for copy in loads:
+        copy.start()
+
     barrier = pltpu.get_barrier_semaphore()
 
     def greet_row(s, carry):
@@ -46,6 +55,9 @@
 
     lax.fori_loop(1, ROWS, greet_row, 0)
     lax.fori_loop(1, COLS, greet_col, 0)
+
+    for copy in loads:
+        copy.wait()
 
     def norm_rows(t, carry):
         rows = pl.ds(pl.multiple_of(t * 256, 256), 256)
@@ -58,7 +70,7 @@
     lax.fori_loop(0, 8, norm_rows, 0)
     w_turned[...] = w_in[...].astype(F32).T.astype(BF16)
     valid = mask[...].astype(F32)
-    valid = jnp.concatenate([valid[16 * b : 16 * b + 16] for b in BLOCK_ORDER], axis=0).T
+    valid = jnp.concatenate([valid.T[16 * b : 16 * b + 16] for b in BLOCK_ORDER], axis=0).T
     mask_rows[...] = jnp.concatenate([valid[0:16], valid[16:32]], axis=1)
 
     def panel_step(kk, carry):
@@ -78,32 +90,40 @@
 
     pl.semaphore_wait(barrier, ROWS + COLS - 2)
 
-    def spread(own, col, send, recv):
+    panels = ((left_own, left_col, send_left, recv_left), (right_own, right_col, send_right, recv_right))
+
+    def spread(which, i):
+        own, col, send, recv = panels[which]
+        q = lax.rem(z + i, 4)
+
         def one(s, carry):
             to = lax.rem(d + s, COLS)
             pltpu.make_async_remote_copy(
-                src_ref=own.at[pl.ds(4 * to, 4)], dst_ref=col.at[:, pl.ds(d * 16, 16), :],
-                send_sem=send, recv_sem=recv, device_id=(z, to), device_id_type=MESH,
+                src_ref=own.at[4 * to + q], dst_ref=col.at[q, pl.ds(d * 16, 16), :],
+                send_sem=send, recv_sem=recv.at[i], device_id=(z, to), device_id_type=MESH,
             ).start()
             return carry
 
         lax.fori_loop(1, COLS, one, 0)
-        pltpu.make_async_copy(own.at[pl.ds(4 * d, 4)], col.at[:, pl.ds(d * 16, 16), :], recv).start()
-
-    spread(left_own, left_col, send_left, recv_left)
-    spread(right_own, right_col, send_right, recv_right)
-
-    def left_copy(q, s):
+        pltpu.make_async_copy(own.at[4 * d + q], col.at[q, pl.ds(d * 16, 16), :], recv.at[i]).start()
+
+    def spread_done(which, i):
+        _, col, _, recv = panels[which]
+        pltpu.make_async_copy(col.at[0], col.at[0], recv.at[i]).wait()
+
+    def left_copy(i, s):
+        q = lax.rem(z + i, 4)
         shift = q + 4 * core
         half, slot, _, _ = place(z, shift, core)
         to = plane_of(shift, half, s)
-        return to, left_col.at[q], left_in.at[slot], send_z.at[2 * q + s], recv_zl
-
-    def right_copy(q, s):
+        return to, left_col.at[q], left_in.at[2 * i + slot // 4], send_z.at[2 * i + s], recv_zl
+
+    def right_copy(i, s):
+        q = lax.rem(z + i, 4)
         shift = q + 4 * core
         _, _, half, slot = place(z, shift, core)
         to = plane_of(shift, s, half)
-        return to, right_turned.at[q], right_in.at[slot], send_z.at[8 + 2 * q + s], recv_zr.at[slot]
+        return to, right_turned.at[q], right_in.at[2 * i + slot // 4], send_z.at[8 + 2 * i + s], recv_zr.at[i]
 
     def launch(to, src, dst, send, recv):
         @pl.when(to != z)
@@ -123,15 +143,18 @@
                 src_ref=src, dst_ref=dst, send_sem=send, recv_sem=recv, device_id=(to, d), device_id_type=MESH
             ).wait_send()
 
-    pltpu.make_async_copy(left_col, left_col, recv_left).wait()
-    for q in range(4):
+    spread(0, 0)
+    spread(0, 1)
+    for chunk in range(8):
+        which, i = chunk // 4, chunk % 4
+        spread_done(which, i)
+        if which == 1:
+            q = lax.rem(z + i, 4)
+            right_turned[q] = right_col[q].astype(F32).T.astype(BF16)
         for s in range(2):
-            launch(*left_copy(q, s))
-    pltpu.make_async_copy(right_col, right_col, recv_right).wait()
-    for q in range(4):
-        right_turned[q] = right_col[q].astype(F32).T.astype(BF16)
-        for s in range(2):
-            launch(*right_copy(q, s))
+            launch(*(right_copy(i, s) if which else left_copy(i, s)))
+        if chunk + 2 < 8:
+            spread((chunk + 2) // 4, (chunk + 2) % 4)
 
     def gate_rows(t, carry):
         rows = pl.ds(pl.multiple_of(t * 256, 256), 256)
@@ -154,58 +177,76 @@
 
     lanes_low = lax.broadcasted_iota(jnp.int32, (32, 128), 1) < 64
 
-    def tile_copy(slot, a):
-        to = lax.rem(left_base + a, ROWS)
-        block = lax.rem(right_base + slot, ROWS)
+    def tile_copy(i, h, a):
+        to = lax.rem(left_base + lax.rem(10 - core - a // 2, 4) + 4 * (a % 2), ROWS)
+        block = lax.rem(right_base + lax.rem(10 - core - i, 4) + 4 * h, ROWS)
         return (
-            to, tiles.at[slot, a], tiles_in.at[my_q, pl.ds(2 * block, 2)], send_t, recv_t
+            to, tiles.at[2 * i + h, a], tiles_in.at[my_q, pl.ds(2 * block, 2)], send_t, recv_t.at[i]
         )
 
-    pltpu.make_async_copy(left_in, left_in, recv_zl).wait()
-
-    def multiply(slot, carry):
-        pltpu.make_async_copy(right_in.at[slot], right_in.at[slot], recv_zr.at[slot]).wait()
+    def multiply(i, h):
+        right = right_in[2 * i + h]
         for pair_index in range(4):
             both = jnp.concatenate([left_in[2 * pair_index], left_in[2 * pair_index + 1]], axis=1)
-            grid = jnp.dot(right_in[slot], both, preferred_element_type=F32)
+            grid = jnp.dot(right, both, preferred_element_type=F32)
             for side in range(2):
                 m = grid[:, 128 * side : 128 * side + 128]
                 kept = jnp.where(lanes_low, m[0:32], m[96:128])
                 moved = jnp.where(lanes_low, m[32:64], m[64:96])
                 tile = (kept + pltpu.roll(moved, 64, axis=1)).astype(BF16)
-                tiles[slot, 2 * pair_index + side] = tile.reshape(2, 16, 128)
-        for a in range(8):
-            launch(*tile_copy(slot, a))
-        return carry
-
-    lax.fori_loop(0, 8, multiply, 0)
-
-    pltpu.make_async_copy(tiles_in, tiles_in, recv_t).wait()
-
-    def return_one(s, carry):
-        to = lax.rem(d + s, COLS)
-        pltpu.make_async_remote_copy(
-            src_ref=tiles_in.at[:, to], dst_ref=gathered.at[pl.ds(4 * d, 4)],
-            send_sem=send_o, recv_sem=recv_o, device_id=(z, to), device_id_type=MESH,
-        ).start()
-        return carry
-
-    lax.fori_loop(1, COLS, return_one, 0)
-    pltpu.make_async_copy(tiles_in.at[:, d], gathered.at[pl.ds(4 * d, 4)], recv_o).start()
+                tiles[2 * i + h, 2 * pair_index + side] = tile.reshape(2, 16, 128)
+                launch(*tile_copy(i, h, 2 * pair_index + side))
+
+    def hand_on(i):
+        pltpu.make_async_copy(tiles_in.at[0], tiles_in.at[0], recv_t.at[i]).wait()
+
+        def one(s, carry):
+            to = lax.rem(d + s, COLS)
+            q = lax.rem(to // 2 + i, 4)
+            pltpu.make_async_remote_copy(
+                src_ref=tiles_in.at[q, to], dst_ref=gathered.at[4 * d + q],
+                send_sem=send_o, recv_sem=recv_o, device_id=(z, to), device_id_type=MESH,
+            ).start()
+            return carry
+
+        lax.fori_loop(1, COLS, one, 0)
+        q = lax.rem(d // 2 + i, 4)
+        pltpu.make_async_copy(tiles_in.at[q, d], gathered.at[4 * d + q], recv_o).start()
+
+    pltpu.make_async_copy(left_in, left_in, recv_zl).wait()
+
+    def step(i, carry):
+        pltpu.make_async_copy(right_in.at[pl.ds(0, 2)], right_in.at[pl.ds(0, 2)], recv_zr.at[i]).wait()
+
+        def half(h, carry):
+            multiply(i, h)
+            return carry
+
+        lax.fori_loop(0, 2, half, 0)
+
+        @pl.when(i > 0)
+        def _():
+            hand_on(i - 1)
+
+        return carry
+
+    lax.fori_loop(0, 4, step, 0)
+    hand_on(3)
 
     pltpu.make_async_copy(left_own.at[pl.ds(0, 124)], left_own.at[pl.ds(0, 124)], send_left).wait()
     pltpu.make_async_copy(right_own.at[pl.ds(0, 124)], right_own.at[pl.ds(0, 124)], send_right).wait()
-    for q in range(4):
+    for i in range(4):
         for s in range(2):
-            landed(*left_copy(q, s))
-            landed(*right_copy(q, s))
-
-    def tile_left(slot, carry):
-        for a in range(8):
-            landed(*tile_copy(slot, a))
-        return carry
-
-    lax.fori_loop(0, 8, tile_left, 0)
+            landed(*left_copy(i, s))
+            landed(*right_copy(i, s))
+
+    def tile_left(i, carry):
+        for h in range(2):
+            for a in range(8):
+                landed(*tile_copy(i, h, a))
+        return carry
+
+    lax.fori_loop(0, 4, tile_left, 0)
 
     pltpu.make_async_copy(gathered, gathered, recv_o).wait()
 
@@ -250,9 +291,19 @@
     out = pl.pallas_call(
         body,
         out_shape=jax.ShapeDtypeStruct((2048, 128), BF16),
-        in_specs=[vmem] * 9,
+        in_specs=[pl.BlockSpec(memory_space=pl.ANY)] * 9,
         out_specs=vmem,
         scratch_shapes=[
+            pltpu.VMEM((2048, 128), BF16),
+            pltpu.VMEM((32, 64), jnp.int32),
+            pltpu.VMEM((1, 128), F32),
+            pltpu.VMEM((1, 128), F32),
+            pltpu.VMEM((128, 512), BF16),
+            pltpu.VMEM((1, 128), F32),
+            pltpu.VMEM((1, 128), F32),
+            pltpu.VMEM((128, 128), BF16),
+            pltpu.VMEM((128, 128), BF16),
+            dma((9,)),
             pltpu.VMEM((2048, 128), F32),
             pltpu.VMEM((2048, 128), F32),
             pltpu.VMEM((2048, 128), F32),
@@ -272,15 +323,15 @@
             pltpu.VMEM((2048, 128), F32),
             pltpu.VMEM((128, 128), F32),
             pltpu.VMEM((128, 128), F32),
-            dma, dma, dma, dma,
-            dma((16,)), dma, dma((8,)),
-            dma, dma, dma, dma,
+            dma, dma, dma((4,)), dma((4,)),
+            dma((16,)), dma, dma((4,)),
+            dma, dma((4,)), dma, dma,
         ],
         compiler_params=pltpu.CompilerParams(
-            collective_id=0, has_side_effects=True, vmem_limit_bytes=40 << 20
+            collective_id=0, has_side_effects=True, vmem_limit_bytes=56 << 20
         ),
     )(
-        pair.reshape(2048, 128), pair_mask, norm_gain.reshape(1, 128), norm_shift.reshape(1, 128), w_in,
+        pair.reshape(2048, 128), pair_mask.T, norm_gain.reshape(1, 128), norm_shift.reshape(1, 128), w_in,
         out_gain.reshape(1, 128), out_shift.reshape(1, 128), w_out, w_gate,
     )
     return out.reshape(64, 32, 128)

time: 126 us -> 116 us (0.921)
  Pallas kernels: 121 us -> 114 us
  local copies, waits for them, and re-layouts: 4.36 us -> 1.87 us
    pallas_call x1, Pallas kernels: 121 us -> 114 us  [on_device(): pl.pallas_call(body, out_shape=jax.ShapeDtypeStruct((2048, 128), BF16), i...]
    unnamed x18 -> x1, local copies, waits for them, and re-layouts: 4.36 us -> 1.87 us
where the time goes in v2:
time: 116 us
  Pallas kernels  114 us (98%)
  local copies, waits for them, and re-layouts  1.87 us (2%)
    pallas_call x1, Pallas kernels, on_device(): pl.pallas_call(body, out_shape=jax.ShapeDtypeStruct((2048, 128), BF16), i...  114 us

profile of v2, /device:TPU:1, one launch (start us, length us, event | category | flops | bytes accessed | tf_op | source)
XLA Modules:
  0.0 116.3 jit_solution(622383483800739087)
XLA Ops:
  0.0 114.4 %shard_map.91 = bf16[2048,128]{1,0:T(8,128)(2,1)} custom-call(bf16[2048,128]{1,0:T(8,128)(2,1)} %bitcast.8, s32[32,64]{1,0:T(8,128)} %bitcast.9, f32[1,128]{1,0:T(1,128)} %bitcast.10, f32[1,128]{1,0:T(1,128)} %bitcast.11, bf16[128,512]{1,0:T(8,128)(2,1)} %w_in_hbm.1, f32[1,128]{1,0:T(1,128)} %bitcast.12, f32[1,128]{1,0:T(1,128)} %bitcast.13, ...), custom_call_target="tpu_custom_call" | custom-call | tf_op jit(solution)/shard_map/pallas_call | solution.py:291
  114.4 1.9 %copy.11 = bf16[64,32,128]{2,1,0:T(8,128)(2,1)} copy(bf16[64,32,128]{2,1,0:T(8,128)(2,1)} %bitcast.7) | data formatting | bytes 1048576

commit v3 on v2

--- a/solution.py
+++ b/solution.py
@@ -8,6 +8,7 @@
 NORM_EPS = 1e-05
 MESH = pl.DeviceIdType.MESH
 ROWS, COLS = 16, 32
+REACH = 6
 F32, BF16 = jnp.float32, jnp.bfloat16
 BLOCK_ORDER = (0, 2, 1, 3)
 
@@ -27,10 +28,10 @@
     pair_hbm, mask_hbm, norm_gain_hbm, norm_shift_hbm, w_in_hbm, out_gain_hbm, out_shift_hbm, w_out_hbm, w_gate_hbm,
     update,
     pair, mask, norm_gain, norm_shift, w_in, out_gain, out_shift, w_out, w_gate, load,
-    normed, wide_left, wide_right, w_turned, mask_rows, left_own, right_own,
-    left_col, right_col, right_turned, left_in, right_in, tiles, tiles_in, gathered, wide_out, gate,
+    normed, wide_left, wide_right, w_turned, mask_rows, own, left_early,
+    col, right_turned, left_in, right_in, tiles, gathered, wide_out, gate,
     gain_col, shift_col,
-    send_left, send_right, recv_left, recv_right, send_z, recv_zl, recv_zr, send_t, recv_t, send_o, recv_o,
+    send_c, recv_c, send_z, recv_zl, recv_zr, send_t, recv_o, send_e, recv_e, send_f,
 ):
     z, d = lax.axis_index("row"), lax.axis_index("col")
     core = lax.rem(d, 2)
@@ -53,7 +54,8 @@
         pl.semaphore_signal(barrier, inc=1, device_id=(z, lax.rem(d + s, COLS)), device_id_type=MESH)
         return carry
 
-    lax.fori_loop(1, ROWS, greet_row, 0)
+    lax.fori_loop(1, REACH + 1, greet_row, 0)
+    lax.fori_loop(ROWS - REACH, ROWS, greet_row, 0)
     lax.fori_loop(1, COLS, greet_col, 0)
 
     for copy in loads:
@@ -85,45 +87,55 @@
         return carry
 
     lax.fori_loop(0, 16, panel_step, 0)
-    left_own[...] = wide_left[...].astype(BF16).reshape(128, 16, 128)
-    right_own[...] = wide_right[...].astype(BF16).reshape(128, 16, 128)
-
-    pl.semaphore_wait(barrier, ROWS + COLS - 2)
-
-    panels = ((left_own, left_col, send_left, recv_left), (right_own, right_col, send_right, recv_right))
-
-    def spread(which, i):
-        own, col, send, recv = panels[which]
+    own[:, :, :, 0] = wide_left[...].astype(BF16).reshape(16, 2, 4, 16, 128)
+    own[:, :, :, 1] = wide_right[...].astype(BF16).reshape(16, 2, 4, 16, 128)
+
+    pl.semaphore_wait(barrier, 2 * REACH + COLS - 1)
+
+    def rank_at(turn):
+        if isinstance(turn, int) and turn in (0, 3):
+            return (0, 0, 0, 2)[turn]
+        late = jnp.where(turn == 3, 2, jnp.where(turn == 1, 1 + 2 * core, 3 - 2 * core))
+        return jnp.where(turn == 0, 0, late)
+
+    def spread(turn):
+        i = rank_at(turn)
         q = lax.rem(z + i, 4)
+        side = 1 if turn == 0 else slice(None)
+        there = col.at[q, side, pl.ds(d * 16, 16), :]
 
         def one(s, carry):
             to = lax.rem(d + s, COLS)
             pltpu.make_async_remote_copy(
-                src_ref=own.at[4 * to + q], dst_ref=col.at[q, pl.ds(d * 16, 16), :],
-                send_sem=send, recv_sem=recv.at[i], device_id=(z, to), device_id_type=MESH,
+                src_ref=own.at[to // 2, to % 2, q, side], dst_ref=there,
+                send_sem=send_c, recv_sem=recv_c.at[i], device_id=(z, to), device_id_type=MESH,
             ).start()
             return carry
 
         lax.fori_loop(1, COLS, one, 0)
-        pltpu.make_async_copy(own.at[4 * d + q], col.at[q, pl.ds(d * 16, 16), :], recv.at[i]).start()
-
-    def spread_done(which, i):
-        _, col, _, recv = panels[which]
-        pltpu.make_async_copy(col.at[0], col.at[0], recv.at[i]).wait()
-
-    def left_copy(i, s):
+        pltpu.make_async_copy(own.at[d // 2, core, q, side], there, recv_c.at[i]).start()
+
+    def spread_done(turn):
+        got = col.at[0, 0] if turn == 0 else col.at[0]
+        pltpu.make_async_copy(got, got, recv_c.at[rank_at(turn)]).wait()
+
+    def left_copy(turn, s):
+        i = rank_at(turn)
         q = lax.rem(z + i, 4)
         shift = q + 4 * core
         half, slot, _, _ = place(z, shift, core)
         to = plane_of(shift, half, s)
-        return to, left_col.at[q], left_in.at[2 * i + slot // 4], send_z.at[2 * i + s], recv_zl
-
-    def right_copy(i, s):
+        send = send_z.at[2 * turn + s]
+        return to, col.at[q, 0], left_in.at[2 * i + slot // 4], send, recv_zl
+
+    def right_copy(turn, s):
+        i = rank_at(turn)
         q = lax.rem(z + i, 4)
         shift = q + 4 * core
         _, _, half, slot = place(z, shift, core)
         to = plane_of(shift, s, half)
-        return to, right_turned.at[q], right_in.at[2 * i + slot // 4], send_z.at[8 + 2 * i + s], recv_zr.at[i]
+        send = send_z.at[8 + 2 * turn + s]
+        return to, right_turned.at[q], right_in.at[2 * i + slot // 4], send, recv_zr.at[i]
 
     def launch(to, src, dst, send, recv):
         @pl.when(to != z)
@@ -143,18 +155,52 @@
                 src_ref=src, dst_ref=dst, send_sem=send, recv_sem=recv, device_id=(to, d), device_id_type=MESH
             ).wait_send()
 
-    spread(0, 0)
-    spread(0, 1)
-    for chunk in range(8):
-        which, i = chunk // 4, chunk % 4
-        spread_done(which, i)
-        if which == 1:
-            q = lax.rem(z + i, 4)
-            right_turned[q] = right_col[q].astype(F32).T.astype(BF16)
+    def early_copy(c, s):
+        q = lax.rem(z, 4)
+        half, slot, _, _ = place(z, q + 4 * c, c)
+        to = plane_of(q + 4 * c, half, s)
+        return to, own.at[:, c, q, 0], left_early.at[slot // 4, c], send_f.at[2 * c + s], recv_e
+
+    def early_out():
+        pltpu.make_async_copy(left_early, left_early, recv_e).wait()
+
+        def one(s, carry):
+            to = lax.rem(d + s, COLS)
+            pltpu.make_async_remote_copy(
+                src_ref=left_early.at[:, to % 2, to // 2], dst_ref=left_in.at[pl.ds(0, 2), pl.ds(d * 16, 16), :],
+                send_sem=send_e, recv_sem=recv_zl, device_id=(z, to), device_id_type=MESH,
+            ).start()
+            return carry
+
+        lax.fori_loop(1, COLS, one, 0)
+        pltpu.make_async_copy(left_early.at[:, core, d // 2], left_in.at[pl.ds(0, 2), pl.ds(d * 16, 16), :], recv_zl).start()
+
+    def send_lefts(turn):
+        spread_done(turn)
         for s in range(2):
-            launch(*(right_copy(i, s) if which else left_copy(i, s)))
-        if chunk + 2 < 8:
-            spread((chunk + 2) // 4, (chunk + 2) % 4)
+            launch(*left_copy(turn, s))
+
+    def send_rights(turn):
+        q = lax.rem(z + rank_at(turn), 4)
+        right_turned[q] = col[q, 1].astype(F32).T.astype(BF16)
+        for s in range(2):
+            launch(*right_copy(turn, s))
+
+    for s in range(2):
+        for c in range(2):
+            launch(*early_copy(c, s))
+    spread(1)
+    spread(2)
+    send_lefts(1)
+    spread(3)
+    send_lefts(2)
+    spread(0)
+    send_lefts(3)
+    early_out()
+    for turn in (1, 2, 3):
+        send_rights(turn)
+    spread_done(0)
+    send_rights(0)
 
     def gate_rows(t, carry):
         rows = pl.ds(pl.multiple_of(t * 256, 256), 256)
@@ -177,12 +223,22 @@
 
     lanes_low = lax.broadcasted_iota(jnp.int32, (32, 128), 1) < 64
 
-    def tile_copy(i, h, a):
-        to = lax.rem(left_base + lax.rem(10 - core - a // 2, 4) + 4 * (a % 2), ROWS)
+    def tile_send(i, h, a, half):
+        row = lax.rem(left_base + lax.rem(10 - core - a // 2, 4) + 4 * (a % 2), ROWS)
         block = lax.rem(right_base + lax.rem(10 - core - i, 4) + 4 * h, ROWS)
-        return (
-            to, tiles.at[2 * i + h, a], tiles_in.at[my_q, pl.ds(2 * block, 2)], send_t, recv_t.at[i]
-        )
+        to = 2 * block + half
+        src, dst = tiles.at[2 * i + h, a, half], gathered.at[4 * d + my_q]
+        here = (row == z) & (to == d)
+
+        @pl.when(jnp.logical_not(here))
+        def _():
+            pltpu.make_async_remote_copy(
+                src_ref=src, dst_ref=dst, send_sem=send_t, recv_sem=recv_o, device_id=(row, to), device_id_type=MESH
+            ).start()
+
+        @pl.when(here)
+        def _():
+            pltpu.make_async_copy(src, dst, recv_o).start()
 
     def multiply(i, h):
         right = right_in[2 * i + h]
@@ -194,59 +250,42 @@
                 kept = jnp.where(lanes_low, m[0:32], m[96:128])
                 moved = jnp.where(lanes_low, m[32:64], m[64:96])
                 tile = (kept + pltpu.roll(moved, 64, axis=1)).astype(BF16)
-                tiles[2 * i + h, 2 * pair_index + side] = tile.reshape(2, 16, 128)
-                launch(*tile_copy(i, h, 2 * pair_index + side))
-
-    def hand_on(i):
-        pltpu.make_async_copy(tiles_in.at[0], tiles_in.at[0], recv_t.at[i]).wait()
-
-        def one(s, carry):
-            to = lax.rem(d + s, COLS)
-            q = lax.rem(to // 2 + i, 4)
-            pltpu.make_async_remote_copy(
-                src_ref=tiles_in.at[q, to], dst_ref=gathered.at[4 * d + q],
-                send_sem=send_o, recv_sem=recv_o, device_id=(z, to), device_id_type=MESH,
-            ).start()
-            return carry
-
-        lax.fori_loop(1, COLS, one, 0)
-        q = lax.rem(d // 2 + i, 4)
-        pltpu.make_async_copy(tiles_in.at[q, d], gathered.at[4 * d + q], recv_o).start()
+                a = 2 * pair_index + side
+                tiles[2 * i + h, a] = tile.reshape(2, 16, 128)
+                for half in range(2):
+                    tile_send(i, h, a, half)
 
     pltpu.make_async_copy(left_in, left_in, recv_zl).wait()
 
-    def step(i, carry):
+    for turn in (1, 2, 3, 0):
+        i = rank_at(turn)
         pltpu.make_async_copy(right_in.at[pl.ds(0, 2)], right_in.at[pl.ds(0, 2)], recv_zr.at[i]).wait()
 
-        def half(h, carry):
+        def half_rank(h, carry, i=i):
             multiply(i, h)
             return carry
 
-        lax.fori_loop(0, 2, half, 0)
-
-        @pl.when(i > 0)
-        def _():
-            hand_on(i - 1)
-
-        return carry
-
-    lax.fori_loop(0, 4, step, 0)
-    hand_on(3)
-
-    pltpu.make_async_copy(left_own.at[pl.ds(0, 124)], left_own.at[pl.ds(0, 124)], send_left).wait()
-    pltpu.make_async_copy(right_own.at[pl.ds(0, 124)], right_own.at[pl.ds(0, 124)], send_right).wait()
-    for i in range(4):
+        lax.fori_loop(0, 2, half_rank, 0)
+
+    def gone(buffer, sem):
+        pltpu.make_async_copy(buffer, buffer, sem).wait()
+
+    gone(col.at[pl.ds(0, 3), :, pl.ds(0, 31 * 16)], send_c)
+    gone(col.at[0, 0, pl.ds(0, 31 * 16)], send_c)
+    gone(left_in.at[pl.ds(0, 2), pl.ds(0, 31 * 16)], send_e)
+    for turn in range(4):
         for s in range(2):
-            landed(*left_copy(i, s))
-            landed(*right_copy(i, s))
-
-    def tile_left(i, carry):
-        for h in range(2):
-            for a in range(8):
-                landed(*tile_copy(i, h, a))
-        return carry
-
-    lax.fori_loop(0, 4, tile_left, 0)
+            landed(*right_copy(turn, s))
+            if turn:
+                landed(*left_copy(turn, s))
+    for s in range(2):
+        for c in range(2):
+            landed(*early_copy(c, s))
+    gone(gathered.at[pl.ds(0, 127)], send_t)
+
+    @pl.when(lax.rem(d // 2 - right_base + 2 * ROWS, ROWS) >= 8)
+    def _():
+        gone(gathered.at[0], send_t)
 
     pltpu.make_async_copy(gathered, gathered, recv_o).wait()
 
@@ -268,7 +307,7 @@
         wide_out[pl.ds(pl.multiple_of(t * 128, 128), 128), :] = block.reshape(128, 128)
         return carry
 
-    lax.fori_loop(0, 16, centre_rows, 0)
+    lax.fori_loop(0, 16, centre_rows, 0, unroll=2)
 
     def project(jj, carry):
         x = wide_out[pl.ds(jj, 128, stride=16), :] * gain_col[...] + shift_col[...]
@@ -279,10 +318,8 @@
                 gate[rows, :] = gate[rows, :] * out[64 * j2 + 16 * s : 64 * j2 + 16 * s + 16]
         return carry
 
-    lax.fori_loop(0, 16, project, 0)
+    lax.fori_loop(0, 16, project, 0, unroll=4)
     update[...] = gate[...].astype(BF16)
-
-    pltpu.make_async_copy(tiles_in.at[:, pl.ds(0, 31)], tiles_in.at[:, pl.ds(0, 31)], send_o).wait()
 
 
 def on_device(pair, pair_mask, norm_gain, norm_shift, w_in, out_gain, out_shift, w_out, w_gate):
@@ -309,23 +346,20 @@
             pltpu.VMEM((2048, 128), F32),
             pltpu.VMEM((512, 128), BF16),
             pltpu.VMEM((16, 128), F32),
-            pltpu.VMEM((128, 16, 128), BF16),
-            pltpu.VMEM((128, 16, 128), BF16),
-            pltpu.VMEM((4, 512, 128), BF16),
-            pltpu.VMEM((4, 512, 128), BF16),
+            pltpu.VMEM((16, 2, 4, 2, 16, 128), BF16),
+            pltpu.VMEM((2, 2, 16, 16, 128), BF16),
+            pltpu.VMEM((4, 2, 512, 128), BF16),
             pltpu.VMEM((4, 128, 512), BF16),
             pltpu.VMEM((8, 512, 128), BF16),
             pltpu.VMEM((8, 128, 512), BF16),
             pltpu.VMEM((8, 8, 2, 16, 128), BF16),
-            pltpu.VMEM((4, 32, 16, 128), BF16),
             pltpu.VMEM((128, 16, 128), BF16),
             pltpu.VMEM((2048, 128), F32),
             pltpu.VMEM((2048, 128), F32),
             pltpu.VMEM((128, 128), F32),
             pltpu.VMEM((128, 128), F32),
-            dma, dma, dma((4,)), dma((4,)),
-            dma((16,)), dma, dma((4,)),
-            dma, dma((4,)), dma, dma,
+            dma, dma((4,)), dma((16,)), dma, dma((4,)),
+            dma, dma, dma, dma, dma((4,)),
         ],
         compiler_params=pltpu.CompilerParams(
             collective_id=0, has_side_effects=True, vmem_limit_bytes=56 << 20

time: 116 us -> 105 us (0.905)
  the two profiles are of different devices: /device:TPU:1 before, /device:TPU:29 now
where the time goes in v3:
time: 105 us
  Pallas kernels  103 us (98%)
  local copies, waits for them, and re-layouts  1.87 us (2%)
    pallas_call x1, Pallas kernels, on_device(): pl.pallas_call(body, out_shape=jax.ShapeDtypeStruct((2048, 128), BF16), i...  103 us

profile of v3, /device:TPU:29, one launch (start us, length us, event | category | flops | bytes accessed | tf_op | source)
XLA Modules:
  0.0 105.2 jit_solution(17574491178813010976)
XLA Ops:
  0.0 103.3 %shard_map.91 = bf16[2048,128]{1,0:T(8,128)(2,1)} custom-call(bf16[2048,128]{1,0:T(8,128)(2,1)} %bitcast.8, s32[32,64]{1,0:T(8,128)} %bitcast.9, f32[1,128]{1,0:T(1,128)} %bitcast.10, f32[1,128]{1,0:T(1,128)} %bitcast.11, bf16[128,512]{1,0:T(8,128)(2,1)} %w_in_hbm.1, f32[1,128]{1,0:T(1,128)} %bitcast.12, f32[1,128]{1,0:T(1,128)} %bitcast.13, ...), custom_call_target="tpu_custom_call" | custom-call | tf_op jit(solution)/shard_map/pallas_call | solution.py:328
  103.3 1.9 %copy.11 = bf16[64,32,128]{2,1,0:T(8,128)(2,1)} copy(bf16[64,32,128]{2,1,0:T(8,128)(2,1)} %bitcast.7) | data formatting | bytes 1048576

commit v4 on v3

--- a/solution.py
+++ b/solution.py
@@ -8,30 +8,29 @@
 NORM_EPS = 1e-05
 MESH = pl.DeviceIdType.MESH
 ROWS, COLS = 16, 32
-REACH = 6
+REACH = 4
 F32, BF16 = jnp.float32, jnp.bfloat16
 BLOCK_ORDER = (0, 2, 1, 3)
 
 
-def place(z, shift, lean):
+def slots(z, shift, lean):
     left = lax.rem(z - shift + 34 - lean, ROWS)
     right = lax.rem(z - shift + 22 - lean, ROWS)
-    return left // 8, lax.rem(left, 8), right // 8, lax.rem(right, 8)
-
-
-def plane_of(shift, left_half, right_half):
-    corner = jnp.where(left_half == 0, right_half, 3 - right_half)
-    return lax.rem(shift + 4 * corner, ROWS)
+    return lax.rem(left, 8), lax.rem(right, 8)
+
+
+HAND_UP = ((1, 2), (1,))
+HAND_DOWN = ((3,), (2, 3))
 
 
 def body(
     pair_hbm, mask_hbm, norm_gain_hbm, norm_shift_hbm, w_in_hbm, out_gain_hbm, out_shift_hbm, w_out_hbm, w_gate_hbm,
     update,
     pair, mask, norm_gain, norm_shift, w_in, out_gain, out_shift, w_out, w_gate, load,
-    normed, wide_left, wide_right, w_turned, mask_rows, own, left_early,
+    normed, wide_left, wide_right, w_turned, mask_rows, own, left_row,
     col, right_turned, left_in, right_in, tiles, gathered, wide_out, gate,
     gain_col, shift_col,
-    send_c, recv_c, send_z, recv_zl, recv_zr, send_t, recv_o, send_e, recv_e, send_f,
+    send_c, recv_c, send_l, recv_l, send_h, send_r, recv_r, send_g, send_t, recv_o, send_e, recv_e,
 ):
     z, d = lax.axis_index("row"), lax.axis_index("col")
     core = lax.rem(d, 2)
@@ -92,115 +91,173 @@
 
     pl.semaphore_wait(barrier, 2 * REACH + COLS - 1)
 
-    def rank_at(turn):
-        if isinstance(turn, int) and turn in (0, 3):
-            return (0, 0, 0, 2)[turn]
-        late = jnp.where(turn == 3, 2, jnp.where(turn == 1, 1 + 2 * core, 3 - 2 * core))
-        return jnp.where(turn == 0, 0, late)
-
-    def spread(turn):
-        i = rank_at(turn)
-        q = lax.rem(z + i, 4)
-        side = 1 if turn == 0 else slice(None)
-        there = col.at[q, side, pl.ds(d * 16, 16), :]
-
-        def one(s, carry):
-            to = lax.rem(d + s, COLS)
-            pltpu.make_async_remote_copy(
-                src_ref=own.at[to // 2, to % 2, q, side], dst_ref=there,
-                send_sem=send_c, recv_sem=recv_c.at[i], device_id=(z, to), device_id_type=MESH,
-            ).start()
-            return carry
-
-        lax.fori_loop(1, COLS, one, 0)
-        pltpu.make_async_copy(own.at[d // 2, core, q, side], there, recv_c.at[i]).start()
-
-    def spread_done(turn):
-        got = col.at[0, 0] if turn == 0 else col.at[0]
-        pltpu.make_async_copy(got, got, recv_c.at[rank_at(turn)]).wait()
-
-    def left_copy(turn, s):
-        i = rank_at(turn)
-        q = lax.rem(z + i, 4)
-        shift = q + 4 * core
-        half, slot, _, _ = place(z, shift, core)
-        to = plane_of(shift, half, s)
-        send = send_z.at[2 * turn + s]
-        return to, col.at[q, 0], left_in.at[2 * i + slot // 4], send, recv_zl
-
-    def right_copy(turn, s):
-        i = rank_at(turn)
-        q = lax.rem(z + i, 4)
-        shift = q + 4 * core
-        _, _, half, slot = place(z, shift, core)
-        to = plane_of(shift, s, half)
-        send = send_z.at[8 + 2 * turn + s]
-        return to, right_turned.at[q], right_in.at[2 * i + slot // 4], send, recv_zr.at[i]
-
-    def launch(to, src, dst, send, recv):
-        @pl.when(to != z)
+    def route(c, i, side, end):
+        shift = lax.rem(z + i, 4) + 4 * c
+        slot = slots(z, shift, c)[side]
+        to = lax.rem(z - slot + 2 - c + 4 * end + ROWS, ROWS)
+        direct = (slot <= 6 - c) if end == 0 else (slot >= 2 - c)
+        outer = (slot < 2 - c) | (slot > 6 - c)
+        return to, 2 * i + slot // 4, direct, outer
+
+    def launch(wanted, to, src, dst, send, recv):
+        @pl.when(wanted & (to != z))
         def _():
             pltpu.make_async_remote_copy(
                 src_ref=src, dst_ref=dst, send_sem=send, recv_sem=recv, device_id=(to, d), device_id_type=MESH
             ).start()
 
-        @pl.when(to == z)
+        @pl.when(wanted & (to == z))
         def _():
             pltpu.make_async_copy(src, dst, recv).start()
 
-    def landed(to, src, dst, send, recv):
-        @pl.when(to != z)
+    def landed(wanted, to, src, dst, send, recv):
+        @pl.when(wanted & (to != z))
         def _():
             pltpu.make_async_remote_copy(
                 src_ref=src, dst_ref=dst, send_sem=send, recv_sem=recv, device_id=(to, d), device_id_type=MESH
             ).wait_send()
 
-    def early_copy(c, s):
-        q = lax.rem(z, 4)
-        half, slot, _, _ = place(z, q + 4 * c, c)
-        to = plane_of(q + 4 * c, half, s)
-        return to, own.at[:, c, q, 0], left_early.at[slot // 4, c], send_f.at[2 * c + s], recv_e
-
-    def early_out():
-        pltpu.make_async_copy(left_early, left_early, recv_e).wait()
+    my_q = lax.rem(z, 4)
+
+    def corner_of(c):
+        return lax.rem(z - my_q - 4 * c + ROWS, ROWS) // 4
+
+    def hands_on(c, i, side):
+        low = lax.rem(corner_of(c) + side, 2) == 0
+        if i in HAND_UP[c] and i in HAND_DOWN[c]:
+            return True, low
+        if i in HAND_UP[c]:
+            return low, low
+        if i in HAND_DOWN[c]:
+            return jnp.logical_not(low), low
+        return None, low
+
+    def hand_copy(low, buffer, at, send, recv):
+        to = lax.rem(z + jnp.where(low, 4, 12), ROWS)
+        place = buffer.at[at]
+        return pltpu.make_async_remote_copy(
+            src_ref=place, dst_ref=place, send_sem=send, recv_sem=recv, device_id=(to, d), device_id_type=MESH
+        )
+
+    def left_copy(c, i, end):
+        to, at, direct, _ = route(c, i, 0, end)
+        return (
+            direct, to, own.at[:, c, lax.rem(z + i, 4), 0], left_row.at[at, c],
+            send_l.at[8 * c + 2 * i + end], recv_l.at[2 * i + c],
+        )
+
+    def left_arrived(c, i):
+        both = left_row.at[pl.ds(0, 2), 0]
+        pltpu.make_async_copy(both, both, recv_l.at[2 * i + c]).wait()
+
+    def left_hand(c, i):
+        _, low = hands_on(c, i, 0)
+        return hand_copy(low, left_row, (2 * i + jnp.where(low, 0, 1), c), send_h.at[2 * i + c], recv_l.at[2 * i + c])
+
+    def left_out(i):
+        for c in range(2):
+            hands, _ = hands_on(c, i, 0)
+            if hands is None:
+                left_arrived(c, i)
+            else:
+
+                @pl.when(jnp.logical_not(hands))
+                def _(c=c):
+                    left_arrived(c, i)
+
+        there = left_in.at[pl.ds(2 * i, 2), pl.ds(d * 16, 16), :]
 
         def one(s, carry):
             to = lax.rem(d + s, COLS)
             pltpu.make_async_remote_copy(
-                src_ref=left_early.at[:, to % 2, to // 2], dst_ref=left_in.at[pl.ds(0, 2), pl.ds(d * 16, 16), :],
-                send_sem=send_e, recv_sem=recv_zl, device_id=(z, to), device_id_type=MESH,
+                src_ref=left_row.at[pl.ds(2 * i, 2), to % 2, to // 2], dst_ref=there,
+                send_sem=send_e, recv_sem=recv_e, device_id=(z, to), device_id_type=MESH,
             ).start()
             return carry
 
         lax.fori_loop(1, COLS, one, 0)
-        pltpu.make_async_copy(left_early.at[:, core, d // 2], left_in.at[pl.ds(0, 2), pl.ds(d * 16, 16), :], recv_zl).start()
-
-    def send_lefts(turn):
-        spread_done(turn)
-        for s in range(2):
-            launch(*left_copy(turn, s))
-
-    def send_rights(turn):
-        q = lax.rem(z + rank_at(turn), 4)
-        right_turned[q] = col[q, 1].astype(F32).T.astype(BF16)
-        for s in range(2):
-            launch(*right_copy(turn, s))
-
-    for s in range(2):
+        pltpu.make_async_copy(left_row.at[pl.ds(2 * i, 2), core, d // 2], there, recv_e).start()
+
+    def spread_right():
+        there = col.at[:, pl.ds(d * 16, 16), :]
+
+        def one(s, carry):
+            to = lax.rem(d + s, COLS)
+            pltpu.make_async_remote_copy(
+                src_ref=own.at[to // 2, to % 2, :, 1], dst_ref=there,
+                send_sem=send_c, recv_sem=recv_c, device_id=(z, to), device_id_type=MESH,
+            ).start()
+            return carry
+
+        lax.fori_loop(1, COLS, one, 0)
+        pltpu.make_async_copy(own.at[d // 2, core, :, 1], there, recv_c).start()
+
+    def on_core(work):
         for c in range(2):
-            launch(*early_copy(c, s))
-    spread(1)
-    spread(2)
-    send_lefts(1)
-    spread(3)
-    send_lefts(2)
-    spread(0)
-    send_lefts(3)
-    early_out()
-    for turn in (1, 2, 3):
-        send_rights(turn)
-    spread_done(0)
-    send_rights(0)
+
+            @pl.when(core == c)
+            def _(c=c):
+                work(c)
+
+    def right_copy(c, i, end):
+        to, at, direct, outer = route(c, i, 1, end)
+        return outer, (
+            direct, to, right_turned.at[lax.rem(z + i, 4)], right_in.at[at], send_r.at[2 * i + end], recv_r.at[i]
+        )
+
+    def right_arrived(i):
+        both = right_in.at[pl.ds(0, 2)]
+        pltpu.make_async_copy(both, both, recv_r.at[i]).wait()
+
+    def right_hand(c, i):
+        _, low = hands_on(c, i, 1)
+        return hand_copy(low, right_in, 2 * i + jnp.where(low, 0, 1), send_g.at[i], recv_r.at[i])
+
+    for i in (1, 3, 2, 0):
+        for end in range(2):
+            for c in range(2):
+                launch(*left_copy(c, i, end))
+    spread_right()
+
+    for i in (1, 3, 2):
+        for c in range(2):
+            hands, _ = hands_on(c, i, 0)
+            if hands is not None:
+
+                @pl.when(hands)
+                def _(c=c, i=i):
+                    left_arrived(c, i)
+                    left_hand(c, i).start()
+
+    pltpu.make_async_copy(col, col, recv_c).wait()
+    for q in range(4):
+        right_turned[q] = col[q].astype(F32).T.astype(BF16)
+
+    def first_rights(c):
+        for i in (1, 3, 2):
+            for end in range(2):
+                outer, (direct, *rest) = right_copy(c, i, end)
+                launch(direct & outer, *rest)
+
+    def other_rights(c):
+        for i in (1, 3, 2, 0):
+            for end in range(2):
+                outer, (direct, *rest) = right_copy(c, i, end)
+                launch(direct & jnp.logical_not(outer), *rest)
+
+    def hand_rights(c):
+        for i in (1, 3, 2):
+            hands, _ = hands_on(c, i, 1)
+            if hands is not None:
+
+                @pl.when(hands)
+                def _(i=i):
+                    right_arrived(i)
+                    right_hand(c, i).start()
+
+    on_core(first_rights)
+    on_core(other_rights)
+    left_out(0)
 
     def gate_rows(t, carry):
         rows = pl.ds(pl.multiple_of(t * 256, 256), 256)
@@ -213,12 +270,15 @@
     gain_col[...] = jnp.broadcast_to(out_gain[...], (128, 128)).T
     shift_col[...] = jnp.broadcast_to(out_shift[...], (128, 128)).T
 
-    my_q = lax.rem(z, 4)
+    for i in (1, 3, 2):
+        left_out(i)
+    on_core(hand_rights)
+
     my_shift = my_q + 4 * core
-    corner = lax.rem(z - my_shift + 16, ROWS) // 4
+    corner = lax.rem(z - my_shift + ROWS, ROWS) // 4
     my_left = corner // 2
     my_right = jnp.where(my_left == 0, corner, 3 - corner)
-    left_base = lax.rem(my_shift - 2 + core + 8 * my_left + 16, ROWS)
+    left_base = lax.rem(my_shift - 2 + core + 8 * my_left + ROWS, ROWS)
     right_base = lax.rem(my_shift + 10 + core + 8 * my_right, ROWS)
 
     lanes_low = lax.broadcasted_iota(jnp.int32, (32, 128), 1) < 64
@@ -255,11 +315,18 @@
                 for half in range(2):
                     tile_send(i, h, a, half)
 
-    pltpu.make_async_copy(left_in, left_in, recv_zl).wait()
-
-    for turn in (1, 2, 3, 0):
-        i = rank_at(turn)
-        pltpu.make_async_copy(right_in.at[pl.ds(0, 2)], right_in.at[pl.ds(0, 2)], recv_zr.at[i]).wait()
+    pltpu.make_async_copy(left_in, left_in, recv_e).wait()
+
+    for i in (1, 3, 2, 0):
+        waiting = jnp.array(True)
+        for c in range(2):
+            hands, _ = hands_on(c, i, 1)
+            if hands is not None:
+                waiting = waiting & jnp.logical_not((core == c) & hands)
+
+        @pl.when(waiting)
+        def _(i=i):
+            right_arrived(i)
 
         def half_rank(h, carry, i=i):
             multiply(i, h)
@@ -270,17 +337,31 @@
     def gone(buffer, sem):
         pltpu.make_async_copy(buffer, buffer, sem).wait()
 
-    gone(col.at[pl.ds(0, 3), :, pl.ds(0, 31 * 16)], send_c)
-    gone(col.at[0, 0, pl.ds(0, 31 * 16)], send_c)
-    gone(left_in.at[pl.ds(0, 2), pl.ds(0, 31 * 16)], send_e)
-    for turn in range(4):
-        for s in range(2):
-            landed(*right_copy(turn, s))
-            if turn:
-                landed(*left_copy(turn, s))
-    for s in range(2):
+    gone(col.at[:, pl.ds(0, 31 * 16)], send_c)
+    gone(left_in.at[:, pl.ds(0, 31 * 16)], send_e)
+    for i in range(4):
         for c in range(2):
-            landed(*early_copy(c, s))
+            for end in range(2):
+                landed(*left_copy(c, i, end))
+            hands, _ = hands_on(c, i, 0)
+            if hands is not None:
+
+                @pl.when(hands)
+                def _(c=c, i=i):
+                    left_hand(c, i).wait_send()
+
+    def rights_gone(c):
+        for i in range(4):
+            for end in range(2):
+                landed(*right_copy(c, i, end)[1])
+            hands, _ = hands_on(c, i, 1)
+            if hands is not None:
+
+                @pl.when(hands)
+                def _(i=i):
+                    right_hand(c, i).wait_send()
+
+    on_core(rights_gone)
     gone(gathered.at[pl.ds(0, 127)], send_t)
 
     @pl.when(lax.rem(d // 2 - right_base + 2 * ROWS, ROWS) >= 8)
@@ -347,8 +428,8 @@
             pltpu.VMEM((512, 128), BF16),
             pltpu.VMEM((16, 128), F32),
             pltpu.VMEM((16, 2, 4, 2, 16, 128), BF16),
-            pltpu.VMEM((2, 2, 16, 16, 128), BF16),
-            pltpu.VMEM((4, 2, 512, 128), BF16),
+            pltpu.VMEM((8, 2, 16, 16, 128), BF16),
+            pltpu.VMEM((4, 512, 128), BF16),
             pltpu.VMEM((4, 128, 512), BF16),
             pltpu.VMEM((8, 512, 128), BF16),
             pltpu.VMEM((8, 128, 512), BF16),
@@ -358,8 +439,9 @@
             pltpu.VMEM((2048, 128), F32),
             pltpu.VMEM((128, 128), F32),
             pltpu.VMEM((128, 128), F32),
-            dma, dma((4,)), dma((16,)), dma, dma((4,)),
-            dma, dma, dma, dma, dma((4,)),
+            dma, dma, dma((16,)), dma((8,)), dma((8,)),
+            dma((8,)), dma((4,)), dma((4,)),
+            dma, dma, dma, dma,
         ],
         compiler_params=pltpu.CompilerParams(
             collective_id=0, has_side_effects=True, vmem_limit_bytes=56 << 20

time: 105 us -> 97.4 us (0.928)
  the two profiles are of different devices: /device:TPU:29 before, /device:TPU:1 now
where the time goes in v4:
time: 97.4 us; the launch traced here: 97 us
  Pallas kernels  95.2 us (98%)
  local copies, waits for them, and re-layouts  1.87 us (2%)
    pallas_call x1, Pallas kernels, on_device(): pl.pallas_call(body, out_shape=jax.ShapeDtypeStruct((2048, 128), BF16), i...  95.2 us

profile of v4, /device:TPU:1, one launch (start us, length us, event | category | flops | bytes accessed | tf_op | source)
XLA Modules:
  0.0 97.0 jit_solution(2240986002903464111)
XLA Ops:
  0.0 95.2 %shard_map.91 = bf16[2048,128]{1,0:T(8,128)(2,1)} custom-call(bf16[2048,128]{1,0:T(8,128)(2,1)} %bitcast.8, s32[32,64]{1,0:T(8,128)} %bitcast.9, f32[1,128]{1,0:T(1,128)} %bitcast.10, f32[1,128]{1,0:T(1,128)} %bitcast.11, bf16[128,512]{1,0:T(8,128)(2,1)} %w_in_hbm.1, f32[1,128]{1,0:T(1,128)} %bitcast.12, f32[1,128]{1,0:T(1,128)} %bitcast.13, ...), custom_call_target="tpu_custom_call" | custom-call | tf_op jit(solution)/shard_map/pallas_call | solution.py:409
  95.2 1.9 %copy.11 = bf16[64,32,128]{2,1,0:T(8,128)(2,1)} copy(bf16[64,32,128]{2,1,0:T(8,128)(2,1)} %bitcast.7) | data formatting | bytes 1048576

commit v5 on v4

--- a/solution.py
+++ b/solution.py
@@ -86,8 +86,11 @@
         return carry
 
     lax.fori_loop(0, 16, panel_step, 0)
-    own[:, :, :, 0] = wide_left[...].astype(BF16).reshape(16, 2, 4, 16, 128)
-    own[:, :, :, 1] = wide_right[...].astype(BF16).reshape(16, 2, 4, 16, 128)
+    for side, wide in enumerate((wide_left, wide_right)):
+        panel = wide[...].astype(BF16).reshape(16, 2, 4, 16, 128)
+        for c in range(2):
+            for q in range(4):
+                own[c, q, side] = panel[:, c, q]
 
     pl.semaphore_wait(barrier, 2 * REACH + COLS - 1)
 
@@ -142,28 +145,31 @@
     def left_copy(c, i, end):
         to, at, direct, _ = route(c, i, 0, end)
         return (
-            direct, to, own.at[:, c, lax.rem(z + i, 4), 0], left_row.at[at, c],
-            send_l.at[8 * c + 2 * i + end], recv_l.at[2 * i + c],
+            direct, to, own.at[c, lax.rem(z + i, 4), 0], left_row.at[at, c],
+            send_l.at[8 * c + 2 * i + end], recv_l.at[2 * at + c],
         )
 
-    def left_arrived(c, i):
-        both = left_row.at[pl.ds(0, 2), 0]
-        pltpu.make_async_copy(both, both, recv_l.at[2 * i + c]).wait()
+    def left_arrived(c, at):
+        block = left_row.at[at, c]
+        pltpu.make_async_copy(block, block, recv_l.at[2 * at + c]).wait()
 
     def left_hand(c, i):
         _, low = hands_on(c, i, 0)
-        return hand_copy(low, left_row, (2 * i + jnp.where(low, 0, 1), c), send_h.at[2 * i + c], recv_l.at[2 * i + c])
+        at = 2 * i + jnp.where(low, 0, 1)
+        return at, hand_copy(low, left_row, (at, c), send_h.at[2 * i + c], recv_l.at[2 * at + c])
 
     def left_out(i):
         for c in range(2):
-            hands, _ = hands_on(c, i, 0)
-            if hands is None:
-                left_arrived(c, i)
-            else:
-
-                @pl.when(jnp.logical_not(hands))
-                def _(c=c):
-                    left_arrived(c, i)
+            hands, low = hands_on(c, i, 0)
+            for h in range(2):
+                if hands is None:
+                    left_arrived(c, 2 * i + h)
+                else:
+                    handed = hands & (jnp.logical_not(low) if h else low)
+
+                    @pl.when(jnp.logical_not(handed))
+                    def _(c=c, h=h):
+                        left_arrived(c, 2 * i + h)
 
         there = left_in.at[pl.ds(2 * i, 2), pl.ds(d * 16, 16), :]
 
@@ -184,13 +190,13 @@
         def one(s, carry):
             to = lax.rem(d + s, COLS)
             pltpu.make_async_remote_copy(
-                src_ref=own.at[to // 2, to % 2, :, 1], dst_ref=there,
+                src_ref=own.at[to % 2, :, 1, to // 2], dst_ref=there,
                 send_sem=send_c, recv_sem=recv_c, device_id=(z, to), device_id_type=MESH,
             ).start()
             return carry
 
         lax.fori_loop(1, COLS, one, 0)
-        pltpu.make_async_copy(own.at[d // 2, core, :, 1], there, recv_c).start()
+        pltpu.make_async_copy(own.at[core, :, 1, d // 2], there, recv_c).start()
 
     def on_core(work):
         for c in range(2):
@@ -202,21 +208,24 @@
     def right_copy(c, i, end):
         to, at, direct, outer = route(c, i, 1, end)
         return outer, (
-            direct, to, right_turned.at[lax.rem(z + i, 4)], right_in.at[at], send_r.at[2 * i + end], recv_r.at[i]
+            direct, to, right_turned.at[lax.rem(z + i, 4)], right_in.at[at], send_r.at[2 * i + end], recv_r.at[at]
         )
 
-    def right_arrived(i):
-        both = right_in.at[pl.ds(0, 2)]
-        pltpu.make_async_copy(both, both, recv_r.at[i]).wait()
+    def right_arrived(at):
+        pltpu.make_async_copy(right_in.at[at], right_in.at[at], recv_r.at[at]).wait()
 
     def right_hand(c, i):
         _, low = hands_on(c, i, 1)
-        return hand_copy(low, right_in, 2 * i + jnp.where(low, 0, 1), send_g.at[i], recv_r.at[i])
-
-    for i in (1, 3, 2, 0):
-        for end in range(2):
-            for c in range(2):
-                launch(*left_copy(c, i, end))
+        at = 2 * i + jnp.where(low, 0, 1)
+        return at, hand_copy(low, right_in, at, send_g.at[i], recv_r.at[at])
+
+    for first in (True, False):
+        for i in (1, 3, 2, 0)[: 3 if first else 4]:
+            for end in range(2):
+                for c in range(2):
+                    outer = route(c, i, 0, end)[3]
+                    direct, *rest = left_copy(c, i, end)
+                    launch(direct & (outer if first else jnp.logical_not(outer)), *rest)
     spread_right()
 
     for i in (1, 3, 2):
@@ -226,8 +235,9 @@
 
                 @pl.when(hands)
                 def _(c=c, i=i):
-                    left_arrived(c, i)
-                    left_hand(c, i).start()
+                    at, copy = left_hand(c, i)
+                    left_arrived(c, at)
+                    copy.start()
 
     pltpu.make_async_copy(col, col, recv_c).wait()
     for q in range(4):
@@ -239,8 +249,8 @@
                 outer, (direct, *rest) = right_copy(c, i, end)
                 launch(direct & outer, *rest)
 
-    def other_rights(c):
-        for i in (1, 3, 2, 0):
+    def other_rights(c, ranks):
+        for i in ranks:
             for end in range(2):
                 outer, (direct, *rest) = right_copy(c, i, end)
                 launch(direct & jnp.logical_not(outer), *rest)
@@ -252,11 +262,12 @@
 
                 @pl.when(hands)
                 def _(i=i):
-                    right_arrived(i)
-                    right_hand(c, i).start()
+                    at, copy = right_hand(c, i)
+                    right_arrived(at)
+                    copy.start()
 
     on_core(first_rights)
-    on_core(other_rights)
+    on_core(lambda c: other_rights(c, (1, 3)))
     left_out(0)
 
     def gate_rows(t, carry):
@@ -270,9 +281,12 @@
     gain_col[...] = jnp.broadcast_to(out_gain[...], (128, 128)).T
     shift_col[...] = jnp.broadcast_to(out_shift[...], (128, 128)).T
 
-    for i in (1, 3, 2):
-        left_out(i)
     on_core(hand_rights)
+    on_core(lambda c: other_rights(c, (2,)))
+    left_out(1)
+    left_out(3)
+    on_core(lambda c: other_rights(c, (0,)))
+    left_out(2)
 
     my_shift = my_q + 4 * core
     corner = lax.rem(z - my_shift + ROWS, ROWS) // 4
@@ -318,15 +332,17 @@
     pltpu.make_async_copy(left_in, left_in, recv_e).wait()
 
     for i in (1, 3, 2, 0):
-        waiting = jnp.array(True)
-        for c in range(2):
-            hands, _ = hands_on(c, i, 1)
-            if hands is not None:
-                waiting = waiting & jnp.logical_not((core == c) & hands)
-
-        @pl.when(waiting)
-        def _(i=i):
-            right_arrived(i)
+        for h in range(2):
+            waiting = jnp.array(True)
+            for c in range(2):
+                hands, low = hands_on(c, i, 1)
+                if hands is not None:
+                    handed = hands & (jnp.logical_not(low) if h else low)
+                    waiting = waiting & jnp.logical_not((core == c) & handed)
+
+            @pl.when(waiting)
+            def _(i=i, h=h):
+                right_arrived(2 * i + h)
 
         def half_rank(h, carry, i=i):
             multiply(i, h)
@@ -348,7 +364,7 @@
 
                 @pl.when(hands)
                 def _(c=c, i=i):
-                    left_hand(c, i).wait_send()
+                    left_hand(c, i)[1].wait_send()
 
     def rights_gone(c):
         for i in range(4):
@@ -359,7 +375,7 @@
 
                 @pl.when(hands)
                 def _(i=i):
-                    right_hand(c, i).wait_send()
+                    right_hand(c, i)[1].wait_send()
 
     on_core(rights_gone)
     gone(gathered.at[pl.ds(0, 127)], send_t)
@@ -427,7 +443,7 @@
             pltpu.VMEM((2048, 128), F32),
             pltpu.VMEM((512, 128), BF16),
             pltpu.VMEM((16, 128), F32),
-            pltpu.VMEM((16, 2, 4, 2, 16, 128), BF16),
+            pltpu.VMEM((2, 4, 2, 16, 16, 128), BF16),
             pltpu.VMEM((8, 2, 16, 16, 128), BF16),
             pltpu.VMEM((4, 512, 128), BF16),
             pltpu.VMEM((4, 128, 512), BF16),
@@ -439,8 +455,8 @@
             pltpu.VMEM((2048, 128), F32),
             pltpu.VMEM((128, 128), F32),
             pltpu.VMEM((128, 128), F32),
-            dma, dma, dma((16,)), dma((8,)), dma((8,)),
-            dma((8,)), dma((4,)), dma((4,)),
+            dma, dma, dma((16,)), dma((16,)), dma((8,)),
+            dma((8,)), dma((8,)), dma((4,)),
             dma, dma, dma, dma,
         ],
         compiler_params=pltpu.CompilerParams(

time: 97.4 us -> 94.9 us (0.974)
  the two profiles are of different devices: /device:TPU:1 before, /device:TPU:13 now
where the time goes in v5:
time: 94.9 us; the launch traced here: 94.8 us
  Pallas kernels  92.9 us (98%)
  local copies, waits for them, and re-layouts  1.87 us (2%)
    pallas_call x1, Pallas kernels, on_device(): pl.pallas_call(body, out_shape=jax.ShapeDtypeStruct((2048, 128), BF16), i...  92.9 us

profile of v5, /device:TPU:13, one launch (start us, length us, event | category | flops | bytes accessed | tf_op | source)
XLA Modules:
  0.0 94.8 jit_solution(2888781922481935130)
XLA Ops:
  0.0 92.9 %shard_map.91 = bf16[2048,128]{1,0:T(8,128)(2,1)} custom-call(bf16[2048,128]{1,0:T(8,128)(2,1)} %bitcast.8, s32[32,64]{1,0:T(8,128)} %bitcast.9, f32[1,128]{1,0:T(1,128)} %bitcast.10, f32[1,128]{1,0:T(1,128)} %bitcast.11, bf16[128,512]{1,0:T(8,128)(2,1)} %w_in_hbm.1, f32[1,128]{1,0:T(1,128)} %bitcast.12, f32[1,128]{1,0:T(1,128)} %bitcast.13, ...), custom_call_target="tpu_custom_call" | custom-call | tf_op jit(solution)/shard_map/pallas_call | solution.py:425
  92.9 1.9 %copy.11 = bf16[64,32,128]{2,1,0:T(8,128)(2,1)} copy(bf16[64,32,128]{2,1,0:T(8,128)(2,1)} %bitcast.7) | data formatting | bytes 1048576

commit v6 on v5

--- a/solution.py
+++ b/solution.py
@@ -228,6 +228,35 @@
                     launch(direct & (outer if first else jnp.logical_not(outer)), *rest)
     spread_right()
 
+    pltpu.make_async_copy(col, col, recv_c).wait()
+    for q in range(4):
+        right_turned[q] = col[q].astype(F32).T.astype(BF16)
+
+    def first_rights(c):
+        for i in (1, 3, 2):
+            for end in range(2):
+                outer, (direct, *rest) = right_copy(c, i, end)
+                launch(direct & outer, *rest)
+
+    def other_rights(c, ranks):
+        for i in ranks:
+            for end in range(2):
+                outer, (direct, *rest) = right_copy(c, i, end)
+                launch(direct & jnp.logical_not(outer), *rest)
+
+    def hand_rights(c):
+        for i in (1, 3, 2):
+            hands, _ = hands_on(c, i, 1)
+            if hands is not None:
+
+                @pl.when(hands)
+                def _(i=i):
+                    at, copy = right_hand(c, i)
+                    right_arrived(at)
+                    copy.start()
+
+    on_core(first_rights)
+    on_core(lambda c: other_rights(c, (1, 3)))
     for i in (1, 3, 2):
         for c in range(2):
             hands, _ = hands_on(c, i, 0)
@@ -239,35 +268,6 @@
                     left_arrived(c, at)
                     copy.start()
 
-    pltpu.make_async_copy(col, col, recv_c).wait()
-    for q in range(4):
-        right_turned[q] = col[q].astype(F32).T.astype(BF16)
-
-    def first_rights(c):
-        for i in (1, 3, 2):
-            for end in range(2):
-                outer, (direct, *rest) = right_copy(c, i, end)
-                launch(direct & outer, *rest)
-
-    def other_rights(c, ranks):
-        for i in ranks:
-            for end in range(2):
-                outer, (direct, *rest) = right_copy(c, i, end)
-                launch(direct & jnp.logical_not(outer), *rest)
-
-    def hand_rights(c):
-        for i in (1, 3, 2):
-            hands, _ = hands_on(c, i, 1)
-            if hands is not None:
-
-                @pl.when(hands)
-                def _(i=i):
-                    at, copy = right_hand(c, i)
-                    right_arrived(at)
-                    copy.start()
-
-    on_core(first_rights)
-    on_core(lambda c: other_rights(c, (1, 3)))
     left_out(0)
 
     def gate_rows(t, carry):

time: 94.9 us -> 93.9 us (0.989)
  the two profiles are of different devices: /device:TPU:13 before, /device:TPU:15 now
where the time goes in v6:
time: 93.9 us; the launch traced here: 93.7 us
  Pallas kernels  91.8 us (98%)
  local copies, waits for them, and re-layouts  1.87 us (2%)
    pallas_call x1, Pallas kernels, on_device(): pl.pallas_call(body, out_shape=jax.ShapeDtypeStruct((2048, 128), BF16), i...  91.8 us

profile of v6, /device:TPU:15, one launch (start us, length us, event | category | flops | bytes accessed | tf_op | source)
XLA Modules:
  0.0 93.7 jit_solution(6846834434538856940)
XLA Ops:
  0.0 91.8 %shard_map.91 = bf16[2048,128]{1,0:T(8,128)(2,1)} custom-call(bf16[2048,128]{1,0:T(8,128)(2,1)} %bitcast.8, s32[32,64]{1,0:T(8,128)} %bitcast.9, f32[1,128]{1,0:T(1,128)} %bitcast.10, f32[1,128]{1,0:T(1,128)} %bitcast.11, bf16[128,512]{1,0:T(8,128)(2,1)} %w_in_hbm.1, f32[1,128]{1,0:T(1,128)} %bitcast.12, f32[1,128]{1,0:T(1,128)} %bitcast.13, ...), custom_call_target="tpu_custom_call" | custom-call | tf_op jit(solution)/shard_map/pallas_call | solution.py:425
  91.9 1.9 %copy.11 = bf16[64,32,128]{2,1,0:T(8,128)(2,1)} copy(bf16[64,32,128]{2,1,0:T(8,128)(2,1)} %bitcast.7) | data formatting | bytes 1048576
